TPU v7x, 128 devices: a whole 4x4x4 slice. The times are simulated.
128 devices in a mesh: exp: 32 (over x_hi, z, y), fsdp: 4 (over x_lo, core).
Axes of the slice: x: 4 (x_hi: 2, x_lo: 2; x = x_hi * 2 + x_lo), y: 4, z: 4, core: 2. Of those that a mesh axis runs over, the one named last changes fastest.
Arguments:
- residual: bfloat16 [128, 4, 7168], P(('fsdp', 'exp')), may hold values from -6 to 6
- gain: float32 [7168], replicated, may hold values from 0.1 to 1.9
- queries: bfloat16 [128, 4, 32, 576], P('fsdp', None, 'exp'), may hold values from -72 to 72
- new_keys: bfloat16 [128, 4, 576], P('fsdp'), may hold values from -6 to 6
- cache: bfloat16 [128, 576, 256], P('fsdp'), may hold values from -6 to 6
- lengths: int32 [128], P('fsdp'), may hold values from 2 to 256, as said below
- w_value: bfloat16 [32, 512, 128], P('exp'), may hold values from -0.25 to 0.25
- w_out: bfloat16 [32, 128, 7168], P('exp'), may hold values from -0.5 to 0.5
- w_gate: bfloat16 [32, 7168, 1024], P(None, 'exp', 'fsdp'), may hold values from -0.0625 to 0.0625
- w_up: bfloat16 [32, 7168, 1024], P(None, 'exp', 'fsdp'), may hold values from -0.0625 to 0.0625
- w_down: bfloat16 [32, 7168, 1024], P(None, 'exp', 'fsdp'), may hold values from -0.1875 to 0.1875
- expert_ids: int32 [128, 4, 8], P(('fsdp', 'exp')), may hold values from 0 to 31, all different within a row; in each aligned block of 4 rows (0 to 3, 4 to 7, ..., all dimensions but the last counted through in order) at most 2 rows name the same one
- gates: float32 [128, 4, 8], P(('fsdp', 'exp')), may hold values from 0.1 to 1
Outputs:
- mixed: float32 [128, 4, 7168], P(('fsdp', 'exp'))
Inputs may be any that keep to these rules, and one draw needn't show every extreme that they name: `expert_ids`: in the 4 rows of one device (aligned blocks of rows and steps in order), no expert is named more than 2 times. `lengths`: some row has exactly 256 cached tokens.
All inputs are finite; a program needn't handle non-finite values.
Results may differ from a plain program's by a relative error of at most 0.006.
Values may be sent and summed in bfloat16 or wider, within the bound.
A program may use at most 128 MiB of HBM per device.

v0:
```python
import jax
import jax.numpy as jnp
from jax import lax
from jax.sharding import PartitionSpec as P

TOP = 8


score_scale = 0.07216878364870322


def expert_share(rows_in, gate_mat, up_mat, down_mat):
    gate_part = jnp.dot(rows_in, gate_mat, preferred_element_type=jnp.float32)
    up_part = jnp.dot(rows_in, up_mat, preferred_element_type=jnp.float32)
    hidden = (jax.nn.silu(gate_part) * up_part).astype(jnp.bfloat16)
    return jnp.einsum("mf,df->md", hidden, down_mat, preferred_element_type=jnp.float32)


def shards(
    residual,
    gain,
    queries,
    new_keys,
    cache,
    lengths,
    w_value,
    w_out,
    w_gate,
    w_up,
    w_down,
    expert_ids,
    gates,
):
    moved = (
        lax.all_to_all(w_gate, "exp", split_axis=0, concat_axis=1, tiled=True),
        lax.all_to_all(w_up, "exp", split_axis=0, concat_axis=1, tiled=True),
        lax.all_to_all(w_down, "exp", split_axis=0, concat_axis=1, tiled=True),
    )
    gate_local = moved[0][0]
    up_local = moved[1][0]
    down_local = moved[2][0]
    query_head = queries[:, :, 0, :]
    group_rows = query_head.shape[0]
    steps = query_head.shape[1]
    latent = w_value.shape[1]
    cache_scores = (
        jnp.einsum("rtc,rcl->rtl", query_head, cache, preferred_element_type=jnp.float32)
        * score_scale
    )
    cache_valid = jnp.arange(cache.shape[2], dtype=jnp.int32)[None, :] < lengths[:, None]
    cache_scores = jnp.where(cache_valid[:, None, :], cache_scores, -1e30)
    new_scores = (
        jnp.einsum("rtc,ruc->rtu", query_head, new_keys, preferred_element_type=jnp.float32)
        * score_scale
    )
    step_index = jnp.arange(steps, dtype=jnp.int32)
    new_valid = step_index[None, :] <= step_index[:, None]
    new_scores = jnp.where(new_valid[None, :, :], new_scores, -1e30)
    highest = jnp.maximum(jnp.max(cache_scores, -1), jnp.max(new_scores, -1))[..., None]
    cache_exp = jnp.exp(cache_scores - highest)
    new_exp = jnp.exp(new_scores - highest)
    total = (jnp.sum(cache_exp, -1) + jnp.sum(new_exp, -1))[..., None]
    cache_weights = (cache_exp / total).astype(jnp.bfloat16)
    new_weights = (new_exp / total).astype(jnp.bfloat16)
    context = jnp.einsum(
        "rtl,rcl->rtc", cache_weights, cache[:, :latent, :], preferred_element_type=jnp.float32
    )
    context = context + jnp.einsum(
        "rtu,ruc->rtc", new_weights, new_keys[:, :, :latent], preferred_element_type=jnp.float32
    )
    context = context.astype(jnp.bfloat16)
    values = jnp.einsum(
        "rtc,cv->rtv", context, w_value[0], preferred_element_type=jnp.float32
    ).astype(jnp.bfloat16)
    values_flat = values.reshape(group_rows * steps, values.shape[2])
    attention = lax.psum_scatter(
        jnp.dot(values_flat, w_out[0], preferred_element_type=jnp.float32),
        "exp",
        scatter_dimension=0,
        tiled=True,
    )
    local_rows = residual.shape[0] * residual.shape[1]
    width = residual.shape[2]
    attended = residual.reshape(local_rows, width).astype(jnp.float32) + attention
    meansq = jnp.mean(attended * attended, -1, keepdims=True)
    normed = (attended * lax.rsqrt(meansq + 1e-06) * gain).astype(jnp.bfloat16)
    experts = lax.axis_size("exp")
    groups = lax.axis_size("fsdp")
    capacity = min(local_rows, 2 * local_rows * TOP // experts)
    flat_ids = expert_ids.reshape(-1)
    hits = (flat_ids[:, None] == jnp.arange(experts, dtype=jnp.int32)[None, :]).astype(jnp.int32)
    earlier = jnp.cumsum(hits, 0) - hits
    position = jnp.sum(earlier * hits, 1)
    target = flat_ids * capacity + position
    slot_index = jnp.arange(experts * capacity, dtype=jnp.int32)
    matches = target.reshape(local_rows, TOP)[:, :, None] == slot_index[None, None, :]
    placing = jnp.sum(matches.astype(jnp.float32), 1).T.astype(jnp.bfloat16)
    combining = jnp.sum(matches.astype(jnp.float32) * gates.reshape(local_rows, TOP)[:, :, None], 1)
    outgoing = jnp.dot(placing, normed, preferred_element_type=jnp.float32).astype(jnp.bfloat16)
    copies = jnp.broadcast_to(
        outgoing.reshape(experts, 1, capacity, width), (experts, groups, capacity, width)
    )
    copies = copies.reshape(experts * groups * capacity, width)
    arrived = lax.all_to_all(copies, ("exp", "fsdp"), split_axis=0, concat_axis=0, tiled=True)
    shares = expert_share(arrived, gate_local, up_local, down_local).astype(jnp.bfloat16)
    returned = lax.all_to_all(shares, ("exp", "fsdp"), split_axis=0, concat_axis=0, tiled=True)
    results = jnp.sum(returned.reshape(experts, groups, capacity, width).astype(jnp.float32), 1)
    results = results.reshape(experts * capacity, width)
    routed = jnp.dot(
        combining, results, preferred_element_type=jnp.float32, precision=lax.Precision.HIGHEST
    )
    mixed = attended + routed
    return mixed.reshape(residual.shape)


def solution(mesh):
    return jax.shard_map(
        shards,
        mesh=mesh,
        in_specs=(
            P(("fsdp", "exp"), None, None),
            P(),
            P("fsdp", None, "exp", None),
            P("fsdp", None, None),
            P("fsdp", None, None),
            P("fsdp"),
            P("exp", None, None),
            P("exp", None, None),
            P(None, "exp", "fsdp"),
            P(None, "exp", "fsdp"),
            P(None, "exp", "fsdp"),
            P(("fsdp", "exp"), None, None),
            P(("fsdp", "exp"), None, None),
        ),
        out_specs=P(("fsdp", "exp"), None, None),
        check_vma=False,
    )
```

profile of v0, /device:TPU:1, one launch (start us, length us, event | category | flops | bytes accessed | tf_op | source)
XLA Modules:
  0.0 634.4 jit_solution(17375389091967374455)
XLA Ops:
  6.5 11.6 %all-to-all-start.3 = ((bf16[32,224,256]{2,1,0:T(8,128)(2,1)}), bf16[32,224,256]{2,1,0:T(8,128)(2,1)}, u32[]{:S(2)}, u32[]{:S(2)}) async-start(bf16[32,224,256]{2,1,0:T(8,128)(2,1)} %param.23), calls=%async_computation.3 | async-start | bytes 7340032 | tf_op jit(solution)/shard_map/all_to_all | solution.py:37
  18.2 0.3 fusion.13
  18.5 0.1 copy.33
  18.6 0.1 fusion.26
  18.9 5.1 fusion.31
  24.1 0.1 fusion.27
  24.3 0.2 fusion.20
  24.6 0.1 copy.38
  24.8 5.7 fusion
  30.5 0.2 fusion.5
  30.7 0.2 convolution_convert_fusion.2
  30.9 2.5 fusion.3
  33.6 33.9 %all-to-all-done.3 = bf16[32,224,256]{2,1,0:T(8,128)(2,1)} async-done(((bf16[32,224,256]{2,1,0:T(8,128)(2,1)}), bf16[32,224,256]{2,1,0:T(8,128)(2,1)}, u32[]{:S(2)}, u32[]{:S(2)}) %all-to-all-start.3) | async-done | bytes 3670048 | tf_op jit(solution)/shard_map/all_to_all | solution.py:37
  67.5 11.5 %all-to-all-start.1 = ((bf16[32,224,256]{2,1,0:T(8,128)(2,1)}), bf16[32,224,256]{2,1,0:T(8,128)(2,1)}, u32[]{:S(2)}, u32[]{:S(2)}) async-start(bf16[32,224,256]{2,1,0:T(8,128)(2,1)} %param.21), calls=%async_computation.1 | async-start | bytes 7340032 | tf_op jit(solution)/shard_map/all_to_all | solution.py:35
  79.2 0.2 select_reduce_fusion.1
  79.5 0.6 dynamic-slice
  80.9 319.5 %all-reduce.3.cloned.1.call-done = f32[128,7168]{1,0:T(8,128)} async-done(((f32[128,7168]{1,0:T(8,128)}), f32[128,7168]{1,0:T(8,128)}) %all-reduce.3.cloned.1.call-update) | async-done | bytes 3670032
  400.3 1.1 multiply_reduce_fusion
  401.5 1.4 convolution_convert_fusion.1
  402.9 0.3 broadcast_in_dim.47
  403.3 1.9 broadcast_in_dim.48
  405.2 77.0 %all_to_all.48 = bf16[128,2,7168]{2,1,0:T(2,128)(2,1)} all-to-all(bf16[128,2,7168]{2,1,0:T(2,128)(2,1)S(1)} %bitcast.50), channel_id=1, replica_groups=mesh['exp'=32,'fsdp'=4] {'exp','fsdp'}, dimensions={0} | all-to-all | bytes 7340032 | tf_op jit(solution)/shard_map/all_to_all | solution.py:104
  482.2 5.9 all-to-all-start.2
  488.1 8.4 %all_to_all.37 = bf16[256,7168]{1,0:T(8,128)(2,1)} reshape(bf16[128,2,7168]{2,1,0:T(2,128)(2,1)} %all_to_all.48) | data formatting | bytes 7340032 | tf_op jit(solution)/shard_map/all_to_all | solution.py:104
  496.5 4.3 fusion.32
  500.8 35.0 %all-to-all-done.2 = bf16[32,224,256]{2,1,0:T(8,128)(2,1)} async-done(((bf16[32,224,256]{2,1,0:T(8,128)(2,1)}), bf16[32,224,256]{2,1,0:T(8,128)(2,1)}, u32[]{:S(2)}, u32[]{:S(2)}) %all-to-all-start.2) | async-done | bytes 3670048 | tf_op jit(solution)/shard_map/all_to_all | solution.py:36
  535.8 10.1 %convolution_convert_fusion = bf16[256,7168]{1,0:T(8,128)(2,1)} fusion(bf16[7168,256]{1,0:T(8,128)(2,1)} %bitcast.11, bf16[256,7168]{1,0:T(8,128)(2,1)} %all_to_all.37, bf16[7168,256]{1,0:T(8,128)(2,1)} %bitcast.10, f32[256,256]{1,0:T(8,128)S(1)} %fusion.32), kind=kOutput, calls=%fused_computation | convolution fusion | flops 1881276416 | bytes 14942208 | tf_op jit(solution)/shard_map/mf,df->md/dot_general | solution.py:16
  545.9 8.1 %all_to_all.41 = bf16[128,2,7168]{2,1,0:T(2,128)(2,1)} reshape(bf16[256,7168]{1,0:T(8,128)(2,1)} %convolution_convert_fusion) | data formatting | bytes 7340032 | tf_op jit(solution)/shard_map/all_to_all | solution.py:106
  554.0 59.0 %all_to_all.49 = bf16[128,2,7168]{2,1,0:T(2,128)(2,1)} all-to-all(bf16[128,2,7168]{2,1,0:T(2,128)(2,1)} %all_to_all.41), channel_id=1, replica_groups=mesh['exp'=32,'fsdp'=4] {'exp','fsdp'}, dimensions={0} | all-to-all | bytes 7340032 | tf_op jit(solution)/shard_map/all_to_all | solution.py:106
  613.0 8.0 %convert_reduce_fusion = f32[32,2,7168]{2,1,0:T(2,128)} fusion(bf16[128,2,7168]{2,1,0:T(2,128)(2,1)} %all_to_all.49), kind=kLoop, calls=%fused_computation.6 | loop fusion | flops 3211264 | bytes 5505024 | tf_op jit(solution)/shard_map/reduce_sum | solution.py:107
  621.0 3.4 reshape.100
  624.4 3.1 fusion.2
  (42 shorter events, 1.1 us)
Async XLA Ops:
  6.5 24.4 %copy-start = (bf16[1,128,7168]{2,1,0:T(8,128)(2,1)S(1)}, bf16[1,128,7168]{2,1,0:T(8,128)(2,1)}, u32[]{:S(2)}) copy-start(bf16[1,128,7168]{2,1,0:T(8,128)(2,1)} %param.20) | copy-start | bytes 5505028
  6.5 11.7 %copy-start.3 = (bf16[32,4,1,576]{3,1,2,0:T(4,128)(2,1)S(1)}, bf16[32,4,1,576]{3,1,2,0:T(4,128)(2,1)}, u32[]{:S(2)}) copy-start(bf16[32,4,1,576]{3,1,2,0:T(4,128)(2,1)} %param.15) | copy-start | bytes 442372
  6.5 11.7 %copy-start.9 = (bf16[32,4,576]{2,1,0:T(4,128)(2,1)S(1)}, bf16[32,4,576]{2,1,0:T(4,128)(2,1)}, u32[]{:S(2)}) copy-start(bf16[32,4,576]{2,1,0:T(4,128)(2,1)} %param.16) | copy-start | bytes 442372
  6.5 12.3 %copy-start.8 = (s32[32]{0:T(128)S(1)}, s32[32]{0:T(128)}, u32[]{:S(2)}) copy-start(s32[32]{0:T(128)} %param.18) | copy-start | bytes 388
  6.5 60.9 %all-to-all-start.3 = ((bf16[32,224,256]{2,1,0:T(8,128)(2,1)}), bf16[32,224,256]{2,1,0:T(8,128)(2,1)}, u32[]{:S(2)}, u32[]{:S(2)}) async-start(bf16[32,224,256]{2,1,0:T(8,128)(2,1)} %param.23), calls=%async_computation.3 | async-start | bytes 7340032 | tf_op jit(solution)/shard_map/all_to_all | solution.py:37
  18.1 382.2 %all-reduce.3.cloned.1.call-start = ((), (), s32[]{:S(2)}) async-start(), calls=%async_computation.5 | async-start | bytes 7340032
  24.8 5.9 copy-start.4
  33.5 45.5 %copy-start.6 = (s32[1,4,8]{2,1,0:T(4,128)S(1)}, s32[1,4,8]{2,1,0:T(4,128)}, u32[]{:S(2)}) copy-start(s32[1,4,8]{2,1,0:T(4,128)} %param.24) | copy-start | bytes 388
  33.5 46.0 %copy-start.10 = (u32[128]{0:T(128)S(1)}, u32[128]{0:T(128)}, u32[]{:S(2)}) copy-start(u32[128]{0:T(128)} %constant.34) | copy-start | bytes 1540
  33.5 47.2 %copy-start.7 = (f32[1,4,8]{2,1,0:T(4,128)S(1)}, f32[1,4,8]{2,1,0:T(4,128)}, u32[]{:S(2)}) copy-start(f32[1,4,8]{2,1,0:T(4,128)} %param.25) | copy-start | bytes 388
  33.5 366.8 %copy-start.2 = (bf16[1,4,7168]{2,1,0:T(4,128)(2,1)S(1)}, bf16[1,4,7168]{2,1,0:T(4,128)(2,1)}, u32[]{:S(2)}) copy-start(bf16[1,4,7168]{2,1,0:T(4,128)(2,1)} %param.13) | copy-start | bytes 172036
  33.6 367.9 %copy-start.5 = (f32[7168]{0:T(1024)S(1)}, f32[7168]{0:T(1024)}, u32[]{:S(2)}) copy-start(f32[7168]{0:T(1024)} %param.14) | copy-start | bytes 86020
  67.5 335.8 %all-to-all-start.1 = ((bf16[32,224,256]{2,1,0:T(8,128)(2,1)}), bf16[32,224,256]{2,1,0:T(8,128)(2,1)}, u32[]{:S(2)}, u32[]{:S(2)}) async-start(bf16[32,224,256]{2,1,0:T(8,128)(2,1)} %param.21), calls=%async_computation.1 | async-start | bytes 7340032 | tf_op jit(solution)/shard_map/all_to_all | solution.py:35
  482.2 53.6 %all-to-all-start.2 = ((bf16[32,224,256]{2,1,0:T(8,128)(2,1)}), bf16[32,224,256]{2,1,0:T(8,128)(2,1)}, u32[]{:S(2)}, u32[]{:S(2)}) async-start(bf16[32,224,256]{2,1,0:T(8,128)(2,1)} %param.22), calls=%async_computation.2 | async-start | bytes 7340032 | tf_op jit(solution)/shard_map/all_to_all | solution.py:36
  613.0 14.5 %copy-start.1 = (bf16[1,128,7168]{2,1,0:T(8,128)(2,1)S(1)}, bf16[1,128,7168]{2,1,0:T(8,128)(2,1)}, u32[]{:S(2)}) copy-start(bf16[1,128,7168]{2,1,0:T(8,128)(2,1)} %param.20) | copy-start | bytes 5505028
Sparse Core Ops, SparseCore 0:
  33.6 366.6 all-reduce.2
where the time goes:
time: 635 us; the launch traced here: 634 us
  waiting for transfers between devices  388 us (61%)
  blocking collectives  136 us (21%)
  matrix products  32.9 us (5%)
  starting transfers between devices  29.1 us (5%)
  local copies, waits for them, and re-layouts  23.6 us (4%)
  between operations  14.3 us (2%)
  other arithmetic  10.1 us (2%)
    unnamed x2, waiting for transfers between devices  320 us
    all_to_all x1, blocking collectives, shards(): lax.all_to_all(copies, ('exp', 'fsdp'), split_axis=0, concat_axis=0, tile...  77 us
    all_to_all x1, blocking collectives, shards(): lax.all_to_all(shares, ('exp', 'fsdp'), split_axis=0, concat_axis=0, tile...  59 us
    all_to_all x1, waiting for transfers between devices, shards(): lax.all_to_all(w_up, 'exp', split_axis=0, concat_axis=1, tiled=True)  35 us
    all_to_all x1, waiting for transfers between devices, shards(): lax.all_to_all(w_down, 'exp', split_axis=0, concat_axis=1, tiled=True)  33.9 us
  transfers between devices with their start and end apart: 4, of which 3 were waited for; matrix products, arithmetic and copies ran while one was open for 4% of the time, Pallas kernels for 0%

commit v1 on v0

v1 whole, which is shorter than its diff:
```python
import functools

import jax
import jax.numpy as jnp
from jax import lax
from jax.experimental import pallas as pl
from jax.experimental.pallas import tpu as pltpu
from jax.sharding import PartitionSpec as P

TOP = 8
score_scale = 0.07216878364870322
MESH = pl.DeviceIdType.MESH
BF = jnp.bfloat16
F32 = jnp.float32
WIDE = 256
HIGH = 56 * 1024 * 1024

NT = (((1,), (1,)), ((), ()))
TN = (((0,), (0,)), ((), ()))


def matmul(a, b):
    return jnp.dot(a, b, preferred_element_type=F32)


def vmem():
    return pl.BlockSpec(memory_space=pltpu.VMEM)


def anywhere():
    return pl.BlockSpec(memory_space=pl.ANY)


def greet(barrier, axis, me, size):
    def one(d, carry):
        pl.semaphore_signal(
            barrier, inc=1, device_id={axis: lax.rem(me + d, size)}, device_id_type=MESH
        )
        return carry

    lax.fori_loop(1, size, one, 0)


def each(lower, upper, body):
    def step(i, carry):
        body(i)
        return carry

    lax.fori_loop(lower, upper, step, 0)


def attend_kernel(
    peers,
    groups,
    q_ref,
    nk_ref,
    cache_ref,
    len_ref,
    wv_ref,
    wo_ref,
    res_ref,
    gain_ref,
    xall_ref,
    att_ref,
    cache_v,
    wo_s,
    new_s,
    ctx_s,
    send_v,
    recv_v,
    ssq_s,
    ssq_r,
    nrm_v,
    cache_sem,
    send_sem,
    recv_sem,
    ssq_send,
    ssq_recv,
    f_send,
    f_recv,
    own_sem,
):
    me = lax.axis_index("exp")
    fs = lax.axis_index("fsdp")
    tokens = q_ref.shape[0]
    latent = wv_ref.shape[0]
    chunks = cache_sem.shape[0]
    per = tokens // chunks
    cache_per = cache_ref.shape[0] // chunks
    width = wo_ref.shape[1] // peers
    barrier = pltpu.get_barrier_semaphore()
    greet(barrier, "exp", me, peers)
    greet(barrier, "fsdp", fs, groups)

    def cache_copy(c):
        rows = pl.ds(c * cache_per, cache_per)
        return pltpu.make_async_copy(cache_ref.at[rows], cache_v.at[rows], cache_sem.at[c])

    for c in range(chunks):
        cache_copy(c).start()

    pad = jnp.zeros((wo_ref.shape[0], WIDE - width), BF)
    for j in range(peers):
        wo_s[j] = jnp.concatenate([wo_ref[:, j * width : (j + 1) * width], pad], axis=1)

    token_r = lax.broadcasted_iota(jnp.int32, (tokens, tokens), 0)
    token_c = lax.broadcasted_iota(jnp.int32, (tokens, tokens), 1)
    same = (token_r // 4 == token_c // 4) & (token_c <= token_r)
    fresh = lax.dot_general(q_ref[...], nk_ref[...], NT, preferred_element_type=F32)
    new_s[...] = jnp.where(same, fresh * score_scale, -1e30)

    def send_copy(c, d):
        peer = lax.rem(me + d, peers)
        rows = pl.ds(pl.multiple_of(c * per, 16), per)
        return pltpu.make_async_remote_copy(
            src_ref=send_v.at[peer, rows],
            dst_ref=recv_v.at[me, rows],
            send_sem=send_sem.at[c, d],
            recv_sem=recv_sem.at[c, me],
            device_id={"exp": peer},
            device_id_type=MESH,
        )

    def recv_copy(c, d):
        peer = lax.rem(me + d, peers)
        rows = pl.ds(pl.multiple_of(c * per, 16), per)
        return pltpu.make_async_remote_copy(
            src_ref=send_v.at[peer, rows],
            dst_ref=recv_v.at[peer, rows],
            send_sem=send_sem.at[c, d],
            recv_sem=recv_sem.at[c, peer],
            device_id={"exp": peer},
            device_id_type=MESH,
        )

    which = lax.broadcasted_iota(jnp.int32, (16, 1), 0) // 4
    lane = lax.broadcasted_iota(jnp.int32, (16, cache_ref.shape[2]), 1)
    mine = (lax.broadcasted_iota(jnp.int32, (per, 1), 0) // 4) + 0

    for c in range(chunks):
        cache_copy(c).wait()

        def block(g, c=c):
            rows = pl.ds(pl.multiple_of(c * per + g * 16, 16), 16)
            first = c * cache_per + g * 4
            q16 = q_ref[rows, :]
            scores = matmul(q16, cache_v[first])
            for i in range(1, 4):
                scores = jnp.where(which == i, matmul(q16, cache_v[first + i]), scores)
            scores = jnp.where(lane < len_ref[rows, :], scores * score_scale, -1e30)
            new = new_s[rows, :]
            highest = jnp.maximum(
                jnp.max(scores, -1, keepdims=True), jnp.max(new, -1, keepdims=True)
            )
            cache_exp = jnp.exp(scores - highest)
            new_exp = jnp.exp(new - highest)
            total = jnp.sum(cache_exp, -1, keepdims=True) + jnp.sum(new_exp, -1, keepdims=True)
            cache_w = (cache_exp / total).astype(BF)
            new_w = (new_exp / total).astype(BF)
            context = lax.dot_general(
                cache_w, cache_v[first, :latent, :], NT, preferred_element_type=F32
            )
            for i in range(1, 4):
                part = lax.dot_general(
                    cache_w, cache_v[first + i, :latent, :], NT, preferred_element_type=F32
                )
                context = jnp.where(which == i, part, context)
            context = context + matmul(new_w, nk_ref[:, :latent])
            ctx_s[pl.ds(pl.multiple_of(g * 16, 16), 16), :] = context.astype(BF)

        each(0, per // 16, block)
        values = matmul(ctx_s[...], wv_ref[...]).astype(BF)
        own_rows = mine + c * (per // 4) == me

        def project(j, c=c, values=values, own_rows=own_rows):
            part = matmul(values, wo_s[j])
            res = jnp.concatenate([res_ref[j]] * (per // 16), axis=0).astype(F32)
            part = part + jnp.where(own_rows, res, 0.0)
            send_v[j, c * per : (c + 1) * per, :] = part.astype(BF)

        each(0, peers, project)
        if c == 0:
            pl.semaphore_wait(barrier, peers - 1 + groups - 1)
        each(1, peers, lambda d, c=c: send_copy(c, d).start())

    def add(d, acc):
        for c in range(chunks):
            recv_copy(c, d).wait_recv()
        return acc + recv_v[lax.rem(me + d, peers)].astype(F32)

    attended = lax.fori_loop(1, peers, add, send_v[me].astype(F32))
    att_ref[...] = attended

    diagonal = token_r == token_c
    column = jnp.sum(attended * attended, -1, keepdims=True)
    row = jnp.sum(jnp.where(diagonal, column, 0.0), 0, keepdims=True)
    ssq_s[...] = jnp.broadcast_to(row, ssq_s.shape)

    def ssq_copy(d, slot):
        peer = lax.rem(me + d, peers)
        return pltpu.make_async_remote_copy(
            src_ref=ssq_s,
            dst_ref=ssq_r.at[slot],
            send_sem=ssq_send.at[d],
            recv_sem=ssq_recv.at[slot],
            device_id={"exp": peer},
            device_id_type=MESH,
        )

    each(1, peers, lambda d: ssq_copy(d, me).start())

    def add_ssq(d, acc):
        slot = lax.rem(me + d, peers)
        ssq_copy(d, slot).wait_recv()
        return acc + ssq_r[slot]

    total = lax.fori_loop(1, peers, add_ssq, ssq_s[...])[:1, :]
    column = jnp.sum(jnp.where(diagonal, total, 0.0), 1, keepdims=True)
    scale = lax.rsqrt(column / (width * peers) + 1e-06)
    nrm_v[...] = (attended * scale * gain_ref[...]).astype(BF)

    own = pltpu.make_async_copy(nrm_v, xall_ref.at[fs], own_sem)
    own.start()

    def group_copy(d, slot):
        return pltpu.make_async_remote_copy(
            src_ref=nrm_v,
            dst_ref=xall_ref.at[slot],
            send_sem=f_send.at[d],
            recv_sem=f_recv.at[slot],
            device_id={"fsdp": lax.rem(fs + d, groups)},
            device_id_type=MESH,
        )

    for d in range(1, groups):
        group_copy(d, fs).start()
    for d in range(1, groups):
        group_copy(d, lax.rem(fs + d, groups)).wait_recv()
    own.wait()

    def finish(d):
        for c in range(chunks):
            send_copy(c, d).wait_send()
        ssq_copy(d, me).wait_send()

    each(1, peers, finish)
    for d in range(1, groups):
        group_copy(d, fs).wait_send()


def attend(q, nk, cache, lens, wv, wo, res, gain, peers, groups):
    tokens = q.shape[0]
    chunks = 4
    per = tokens // chunks
    return pl.pallas_call(
        functools.partial(attend_kernel, peers, groups),
        out_shape=(
            jax.ShapeDtypeStruct((groups, tokens, WIDE), BF),
            jax.ShapeDtypeStruct((tokens, WIDE), F32),
        ),
        in_specs=[vmem(), vmem(), anywhere()] + [vmem()] * 5,
        out_specs=(anywhere(), vmem()),
        scratch_shapes=[
            pltpu.VMEM(cache.shape, BF),
            pltpu.VMEM((peers, wo.shape[0], WIDE), BF),
            pltpu.VMEM((tokens, tokens), F32),
            pltpu.VMEM((per, wv.shape[0]), BF),
            pltpu.VMEM((peers, tokens, WIDE), BF),
            pltpu.VMEM((peers, tokens, WIDE), BF),
            pltpu.VMEM((8, tokens), F32),
            pltpu.VMEM((peers, 8, tokens), F32),
            pltpu.VMEM((tokens, WIDE), BF),
            pltpu.SemaphoreType.DMA((chunks,)),
            pltpu.SemaphoreType.DMA((chunks, peers)),
            pltpu.SemaphoreType.DMA((chunks, peers)),
            pltpu.SemaphoreType.DMA((peers,)),
            pltpu.SemaphoreType.DMA((peers,)),
            pltpu.SemaphoreType.DMA((groups,)),
            pltpu.SemaphoreType.DMA((groups,)),
            pltpu.SemaphoreType.DMA,
        ],
        compiler_params=pltpu.CompilerParams(
            collective_id=0, has_side_effects=True, vmem_limit_bytes=HIGH
        ),
        name="attend",
    )(q, nk, cache, lens, wv, wo, res, gain)


def gate_up_kernel(lo_ref, hi_ref, x_ref, pos_ref, wg_ref, wu_ref, out_ref, acc):
    tiles, rows, wide = out_ref.shape
    half = wide // 2
    tokens = x_ref.shape[0]
    depth = wg_ref.shape[1]
    line = lax.broadcasted_iota(jnp.int32, (rows, tokens), 0)

    def tile(t):
        acc[...] = jnp.zeros_like(acc)

        def visit(e):
            place = (pos_ref[e] - t * rows == line).astype(F32).astype(BF)
            picked = matmul(place, x_ref[...]).astype(BF)[:, :depth]
            acc[:, :half] += matmul(picked, wg_ref[e])
            acc[:, half:] += matmul(picked, wu_ref[e])

        each(lo_ref[t], hi_ref[t], visit)
        out_ref[t] = acc[...].astype(BF)

    each(0, tiles, tile)


def gate_up(lo, hi, x, pos, wg, wu, tiles, rows):
    smem = pl.BlockSpec(memory_space=pltpu.SMEM)
    return pl.pallas_call(
        gate_up_kernel,
        out_shape=jax.ShapeDtypeStruct((tiles, rows, 2 * wg.shape[2]), BF),
        in_specs=[smem, smem] + [vmem()] * 4,
        out_specs=vmem(),
        scratch_shapes=[pltpu.VMEM((rows, 2 * wg.shape[2]), F32)],
        compiler_params=pltpu.CompilerParams(vmem_limit_bytes=HIGH),
        name="gate_up",
    )(lo, hi, x, pos, wg, wu)


def hidden_kernel(peers, part_ref, hid_ref, recv_v, acc, hid_v, r_send, r_recv, g_send, g_recv, own_sem):
    me = lax.axis_index("exp")
    half = hid_v.shape[1]
    barrier = pltpu.get_barrier_semaphore()
    greet(barrier, "exp", me, peers)
    own = pltpu.make_async_copy(part_ref.at[me], recv_v.at[me], own_sem.at[0])
    own.start()
    pl.semaphore_wait(barrier, peers - 1)

    def part_copy(d, slot):
        peer = lax.rem(me + d, peers)
        return pltpu.make_async_remote_copy(
            src_ref=part_ref.at[peer],
            dst_ref=recv_v.at[slot],
            send_sem=r_send.at[d],
            recv_sem=r_recv.at[slot],
            device_id={"exp": peer},
            device_id_type=MESH,
        )

    each(1, peers, lambda d: part_copy(d, me).start())
    own.wait()
    acc[...] = recv_v[me].astype(F32)

    def add(d):
        slot = lax.rem(me + peers - d, peers)
        part_copy(d, slot).wait_recv()
        acc[...] += recv_v[slot].astype(F32)

    each(1, peers, add)
    gate = acc[:, :half]
    hid_v[...] = (gate / (1.0 + jnp.exp(-gate)) * acc[:, half:]).astype(BF)

    def hid_copy(d, slot):
        peer = lax.rem(me + d, peers)
        return pltpu.make_async_remote_copy(
            src_ref=hid_v,
            dst_ref=hid_ref.at[slot],
            send_sem=g_send.at[d],
            recv_sem=g_recv.at[slot],
            device_id={"exp": peer},
            device_id_type=MESH,
        )

    own = pltpu.make_async_copy(hid_v, hid_ref.at[me], own_sem.at[1])
    own.start()
    each(1, peers, lambda d: hid_copy(d, me).start())
    own.wait()

    def finish(d):
        part_copy(d, me).wait_send()
        hid_copy(d, lax.rem(me + peers - d, peers)).wait_recv()
        hid_copy(d, me).wait_send()

    each(1, peers, finish)


def hidden(part, peers):
    tiles, rows, wide = part.shape
    return pl.pallas_call(
        functools.partial(hidden_kernel, peers),
        out_shape=jax.ShapeDtypeStruct((tiles, rows, wide // 2), BF),
        in_specs=[anywhere()],
        out_specs=anywhere(),
        scratch_shapes=[
            pltpu.VMEM((peers, rows, wide), BF),
            pltpu.VMEM((rows, wide), F32),
            pltpu.VMEM((rows, wide // 2), BF),
            pltpu.SemaphoreType.DMA((peers,)),
            pltpu.SemaphoreType.DMA((peers,)),
            pltpu.SemaphoreType.DMA((peers,)),
            pltpu.SemaphoreType.DMA((peers,)),
            pltpu.SemaphoreType.DMA((2,)),
        ],
        compiler_params=pltpu.CompilerParams(
            collective_id=1, has_side_effects=True, vmem_limit_bytes=HIGH
        ),
        name="hidden",
    )(part)


def down_kernel(lo_ref, hi_ref, hid_ref, pos_ref, gate_ref, wd_ref, out_ref, acc):
    tiles, rows, _ = hid_ref.shape
    tokens = pos_ref.shape[2]
    depth = wd_ref.shape[1]
    line = lax.broadcasted_iota(jnp.int32, (rows, tokens), 0)
    acc[...] = jnp.zeros_like(acc)

    def tile(t):
        def visit(e):
            hit = pos_ref[e] - t * rows == line
            share = lax.dot_general(hid_ref[t], wd_ref[e], NT, preferred_element_type=F32)
            weight = jnp.sum(jnp.where(hit, gate_ref[e], 0.0), 1, keepdims=True)
            share = (share * weight).astype(BF)
            acc[:, :depth] += lax.dot_general(
                hit.astype(F32).astype(BF), share, TN, preferred_element_type=F32
            )

        each(lo_ref[t], hi_ref[t], visit)

    each(0, tiles, tile)
    out_ref[...] = acc[...].astype(BF)


def down(lo, hi, hid, pos, gate, wd):
    smem = pl.BlockSpec(memory_space=pltpu.SMEM)
    tokens = pos.shape[2]
    return pl.pallas_call(
        down_kernel,
        out_shape=jax.ShapeDtypeStruct((tokens, WIDE), BF),
        in_specs=[smem, smem] + [vmem()] * 4,
        out_specs=vmem(),
        scratch_shapes=[pltpu.VMEM((tokens, WIDE), F32)],
        compiler_params=pltpu.CompilerParams(vmem_limit_bytes=HIGH),
        name="down",
    )(lo, hi, hid, pos, gate, wd)


def finish_kernel(
    peers, groups, routed_ref, att_ref, out_ref, recv_v, send_v, f_send, f_recv, o_send, o_recv, own_sem
):
    me = lax.axis_index("exp")
    fs = lax.axis_index("fsdp")
    own_rows = send_v.shape[1]
    barrier = pltpu.get_barrier_semaphore()
    greet(barrier, "exp", me, peers)
    greet(barrier, "fsdp", fs, groups)
    pl.semaphore_wait(barrier, peers - 1 + groups - 1)

    def group_copy(d, slot):
        peer = lax.rem(fs + d, groups)
        return pltpu.make_async_remote_copy(
            src_ref=routed_ref.at[peer],
            dst_ref=recv_v.at[slot],
            send_sem=f_send.at[d],
            recv_sem=f_recv.at[slot],
            device_id={"fsdp": peer},
            device_id_type=MESH,
        )

    for d in range(1, groups):
        group_copy(d, fs).start()
    mixed = att_ref[...] + routed_ref[fs].astype(F32)
    for d in range(1, groups):
        slot = lax.rem(fs + d, groups)
        group_copy(d, slot).wait_recv()
        mixed = mixed + recv_v[slot].astype(F32)
    for j in range(peers):
        send_v[j] = mixed[j * own_rows : (j + 1) * own_rows, :]

    def out_copy(d, slot):
        peer = lax.rem(me + d, peers)
        return pltpu.make_async_remote_copy(
            src_ref=send_v.at[peer],
            dst_ref=out_ref.at[slot],
            send_sem=o_send.at[d],
            recv_sem=o_recv.at[slot],
            device_id={"exp": peer},
            device_id_type=MESH,
        )

    own = pltpu.make_async_copy(send_v.at[me], out_ref.at[me], own_sem)
    own.start()
    each(1, peers, lambda d: out_copy(d, me).start())
    own.wait()

    def close(d):
        out_copy(d, lax.rem(me + peers - d, peers)).wait_recv()
        out_copy(d, me).wait_send()

    each(1, peers, close)
    for d in range(1, groups):
        group_copy(d, fs).wait_send()


def finish(routed, att, peers, groups):
    tokens = att.shape[0]
    return pl.pallas_call(
        functools.partial(finish_kernel, peers, groups),
        out_shape=jax.ShapeDtypeStruct((peers, tokens // peers, WIDE), F32),
        in_specs=[vmem(), vmem()],
        out_specs=anywhere(),
        scratch_shapes=[
            pltpu.VMEM((groups, tokens, WIDE), BF),
            pltpu.VMEM((peers, tokens // peers, WIDE), F32),
            pltpu.SemaphoreType.DMA((groups,)),
            pltpu.SemaphoreType.DMA((groups,)),
            pltpu.SemaphoreType.DMA((peers,)),
            pltpu.SemaphoreType.DMA((peers,)),
            pltpu.SemaphoreType.DMA,
        ],
        compiler_params=pltpu.CompilerParams(
            collective_id=2, has_side_effects=True, vmem_limit_bytes=HIGH
        ),
        name="finish",
    )(routed, att)


def routing(expert_ids, gates, experts, tiles, rows):
    ids = expert_ids.reshape(-1, TOP)
    flat = jnp.concatenate([ids.astype(F32), gates.reshape(-1, TOP)], axis=1)
    everyone = lax.all_gather(flat, ("fsdp", "exp"), axis=0, tiled=True)
    ids = everyone[:, :TOP].astype(jnp.int32)
    chosen = ids[:, :, None] == jnp.arange(experts, dtype=jnp.int32)[None, None, :]
    gate = jnp.sum(jnp.where(chosen, everyone[:, TOP:, None], 0.0), 1)
    hits = jnp.any(chosen, 1)
    tokens = ids.shape[0]
    order = jnp.arange(tokens, dtype=jnp.int32)
    before = (order[None, :] < order[:, None]).astype(BF)
    rank = matmul(before, hits.astype(BF)).astype(jnp.int32)
    counts = jnp.sum(hits.astype(jnp.int32), 0)
    numbers = jnp.arange(experts, dtype=jnp.int32)
    starts = jnp.sum(jnp.where(numbers[None, :] < numbers[:, None], counts[None, :], 0), 1)
    ends = starts + counts
    pos = jnp.where(hits, rank + starts[None, :], -1)
    edge = jnp.arange(tiles, dtype=jnp.int32) * rows
    lo = jnp.sum((ends[None, :] <= edge[:, None]).astype(jnp.int32), 1)
    hi = jnp.sum((starts[None, :] < edge[:, None] + rows).astype(jnp.int32), 1)
    return lo, hi, pos.T.reshape(experts, 1, tokens), gate.T.reshape(experts, 1, tokens)


def shards(
    residual,
    gain,
    queries,
    new_keys,
    cache,
    lengths,
    w_value,
    w_out,
    w_gate,
    w_up,
    w_down,
    expert_ids,
    gates,
):
    peers = lax.axis_size("exp")
    groups = lax.axis_size("fsdp")
    group_rows, steps, _, key = queries.shape
    tokens = group_rows * steps
    model = residual.shape[2]
    width = model // peers
    experts = w_gate.shape[0]
    pairs = tokens * groups * TOP
    rows = pairs // peers

    lo, hi, pos, gate = routing(expert_ids, gates, experts, peers, rows)

    res = residual.reshape(steps, peers, width).transpose(1, 0, 2)
    res = jnp.pad(jnp.tile(res, (1, 16 // steps, 1)), ((0, 0), (0, 0), (0, WIDE - width)))
    own_gain = lax.dynamic_slice(gain, (lax.axis_index("exp") * width,), (width,))
    own_gain = jnp.pad(own_gain, (0, WIDE - width)).reshape(1, WIDE)
    lens = jnp.repeat(lengths, steps).reshape(tokens, 1)
    xall, att = attend(
        queries.reshape(tokens, key),
        new_keys.reshape(tokens, key),
        cache,
        lens,
        w_value[0],
        w_out[0],
        res,
        own_gain,
        peers,
        groups,
    )
    part = gate_up(
        lo, hi, xall.reshape(groups * tokens, WIDE), pos, w_gate, w_up, peers, rows
    )
    hid = hidden(part, peers)
    routed = down(lo, hi, hid, pos, gate, w_down)
    out = finish(routed.reshape(groups, tokens, WIDE), att, peers, groups)
    return out[:, :, :width].transpose(1, 0, 2).reshape(residual.shape)


def solution(mesh):
    return jax.shard_map(
        shards,
        mesh=mesh,
        in_specs=(
            P(("fsdp", "exp"), None, None),
            P(),
            P("fsdp", None, "exp", None),
            P("fsdp", None, None),
            P("fsdp", None, None),
            P("fsdp"),
            P("exp", None, None),
            P("exp", None, None),
            P(None, "exp", "fsdp"),
            P(None, "exp", "fsdp"),
            P(None, "exp", "fsdp"),
            P(("fsdp", "exp"), None, None),
            P(("fsdp", "exp"), None, None),
        ),
        out_specs=P(("fsdp", "exp"), None, None),
        check_vma=False,
    )
```

time: 635 us -> 579 us (0.912)
  waiting for transfers between devices: 388 us -> 0 us
  Pallas kernels: 0 us -> 238 us
  blocking collectives: 136 us -> 326 us
  matrix products: 32.9 us -> 0.26 us
  starting transfers between devices: 29.1 us -> 0 us
  between operations: 14.3 us -> 0.1 us
  local copies, waits for them, and re-layouts: 23.6 us -> 11.5 us
  other arithmetic: 10.1 us -> 2.59 us
    all_gather x0 -> x1, blocking collectives: none -> 326 us  [routing(): everyone = lax.all_gather(flat, ('fsdp', 'exp'), axis=0, tiled=True)]
    unnamed x2 -> x0, waiting for transfers between devices: 320 us -> none
    pallas_call x0 -> x5, Pallas kernels: none -> 238 us  [the longest x1 84.7 us: hidden(): pl.pallas_call(functools.partial(hidden_kernel, peers), out_shape=jax.Sha...]
    all_to_all x2 -> x0, blocking collectives: 136 us -> none  [the longest x1 77 us: shards(): lax.all_to_all(copies, ('exp', 'fsdp'), split_axis=0, concat_axis=0, tile...]
    all_to_all x3 -> x0, waiting for transfers between devices: 68.9 us -> none  [the longest x1 35 us: shards(): lax.all_to_all(w_up, 'exp', split_axis=0, concat_axis=1, tiled=True)]
    dot_general x10 -> x1, matrix products: 32.9 us -> 0.26 us  [matmul(): return jnp.dot(a, b, preferred_element_type=F32)]
    all_to_all x3 -> x0, starting transfers between devices: 29 us -> none  [the longest x1 11.6 us: shards(): lax.all_to_all(w_down, 'exp', split_axis=0, concat_axis=1, tiled=True)]
    all_to_all x2 -> x0, local copies, waits for them, and re-layouts: 16.5 us -> none  [the longest x1 8.41 us: shards(): lax.all_to_all(copies, ('exp', 'fsdp'), split_axis=0, concat_axis=0, tile...]
  transfers between devices with their start and end apart: 4 -> 0, of which waited for: 3 -> 0; matrix products, arithmetic and copies ran while one was open for 4% -> 0% of each run, Pallas kernels for 0% -> 0%
where the time goes in v1:
time: 579 us; the launch traced here: 578 us
  blocking collectives  326 us (56%)
  Pallas kernels  238 us (41%)
  local copies, waits for them, and re-layouts  11.5 us (2%)
    all_gather x1, blocking collectives, routing(): everyone = lax.all_gather(flat, ('fsdp', 'exp'), axis=0, tiled=True)  326 us
    pallas_call x1, Pallas kernels, hidden(): pl.pallas_call(functools.partial(hidden_kernel, peers), out_shape=jax.Sha...  84.7 us
    pallas_call x1, Pallas kernels, attend(): pl.pallas_call(functools.partial(attend_kernel, peers, groups), out_shape...  57.8 us
    pallas_call x1, Pallas kernels, finish(): pl.pallas_call(functools.partial(finish_kernel, peers, groups), out_shape...  34.8 us
    pallas_call x1, Pallas kernels, down(): pl.pallas_call(down_kernel, out_shape=jax.ShapeDtypeStruct((tokens, WIDE)...  31.4 us
    pallas_call x1, Pallas kernels, gate_up(): pl.pallas_call(gate_up_kernel, out_shape=jax.ShapeDtypeStruct((tiles, row...  29.3 us

profile of v1, /device:TPU:1, one launch (start us, length us, event | category | flops | bytes accessed | tf_op | source)
XLA Modules:
  0.0 578.3 jit_solution(12457090005731009698)
XLA Ops:
  0.0 0.8 dynamic_slice.3
  0.8 0.6 pad.9
  1.4 0.7 convert_bitcast_fusion
  2.1 0.8 maximum_bitcast_fusion
  2.8 0.7 broadcast_in_dim.46
  3.5 0.7 reshape_reshape.4.len_ref
  4.2 0.9 reshape.56
  5.2 0.1 copy.32
  5.3 1.7 reshape.54.q_ref
  6.9 1.6 reshape.55.nk_ref
  8.6 0.1 tile.4
  8.6 0.2 tile.10
  8.8 0.7 pad.8.res_ref
  9.5 57.8 %attend.1 = (bf16[4,128,256]{2,1,0:T(8,128)(2,1)}, f32[128,256]{1,0:T(8,128)}) custom-call(bf16[128,576]{1,0:T(8,128)(2,1)} %reshape.54.q_ref, bf16[128,576]{1,0:T(8,128)(2,1)} %reshape.55.nk_ref, bf16[32,576,256]{2,1,0:T(8,128)(2,1)} %cache_ref.1, s32[128,1]{1,0:T(8,128)} %reshape_reshape.4.len_ref, bf16[512,128]{1,0:T(8,128)(2,1)} %bitcast.26, ...), custom_call_target="tpu_custom_call" | custom-call | tf_op jit(solution)/shard_map/attend/pallas_call | solution.py:255
  67.4 325.8 %all-gather = f32[128,4,16]{2,1,0:T(4,128)S(1)} all-gather(f32[1,4,16]{2,1,0:T(4,128)S(1)} %maximum_bitcast_fusion), channel_id=1, replica_groups=mesh['exp'=32,'fsdp'=4] {'fsdp','exp'}, dimensions={0}, use_global_device_ids=true | all-gather | bytes 33024 | tf_op jit(solution)/shard_map/all_gather | solution.py:525
  393.2 0.1 fusion.3
  393.3 0.1 copy.34
  393.4 0.1 copy.36
  393.5 0.1 fusion.2
  393.6 0.1 convert_reduce_fusion
  393.7 0.1 select_reduce_fusion.1
  393.9 0.8 convert_reduce_fusion.1
  394.6 0.1 select_reduce_fusion
  394.7 0.7 reshape.60.gate_ref
  395.4 0.3 fusion.1
  395.6 0.7 reshape.59.pos_ref
  396.3 29.3 %gate_up.1.part_ref = bf16[32,128,512]{2,1,0:T(8,128)(2,1)} custom-call(s32[32]{0:T(128)} %get-tuple-element.12.lo_ref, s32[32]{0:T(128)} %get-tuple-element.11.hi_ref, bf16[512,256]{1,0:T(8,128)(2,1)} %bitcast.23, s32[32,1,512]{2,1,0:T(1,128)} %reshape.59.pos_ref, bf16[32,224,256]{2,1,0:T(8,128)(2,1)} %wg_ref.1, bf16[32,224,256]{2,1,0:T(8,128)(2,1)} %wu_ref.1), custom_call_target="tpu_custom_call" | custom-call | tf_op jit(solution)/shard_map/gate_up/pallas_call | solution.py:313
  425.6 84.7 %hidden.1.hid_ref = bf16[32,128,256]{2,1,0:T(8,128)(2,1)} custom-call(bf16[32,128,512]{2,1,0:T(8,128)(2,1)} %gate_up.1.part_ref), custom_call_target="tpu_custom_call" | custom-call | tf_op jit(solution)/shard_map/hidden/pallas_call | solution.py:383
  510.3 31.4 %down.1 = bf16[512,256]{1,0:T(8,128)(2,1)} custom-call(s32[32]{0:T(128)} %get-tuple-element.12.lo_ref, s32[32]{0:T(128)} %get-tuple-element.11.hi_ref, bf16[32,128,256]{2,1,0:T(8,128)(2,1)} %hidden.1.hid_ref, s32[32,1,512]{2,1,0:T(1,128)} %reshape.59.pos_ref, f32[32,1,512]{2,1,0:T(1,128)} %reshape.60.gate_ref, bf16[32,224,256]{2,1,0:T(8,128)(2,1)} %wd_ref.1), custom_call_target="tpu_custom_call" | custom-call | tf_op jit(solution)/shard_map/down/pallas_call | solution.py:431
  541.7 34.8 %finish.1 = f32[32,4,256]{2,1,0:T(4,128)} custom-call(bf16[4,128,256]{2,1,0:T(8,128)(2,1)} %bitcast.22, f32[128,256]{1,0:T(8,128)} %get-tuple-element.8.att_ref), custom_call_target="tpu_custom_call" | custom-call | tf_op jit(solution)/shard_map/finish/pallas_call | solution.py:501
  576.5 0.9 slice_bitcast_fusion
  577.5 0.8 reshape.62
  (5 shorter events, 0.0 us)

commit v2 on v0

v2 whole, which is shorter than its diff:
```python
import functools

import jax
import jax.numpy as jnp
from jax import lax
from jax.experimental import pallas as pl
from jax.experimental.pallas import tpu as pltpu
from jax.sharding import PartitionSpec as P

TOP = 8
STEPS = 4
score_scale = 0.07216878364870322
MESH = pl.DeviceIdType.MESH
BF = jnp.bfloat16
F32 = jnp.float32
WIDE = 256
HIGH = 58 * 1024 * 1024
NX, NZ, NY = 2, 4, 4
NT = (((1,), (1,)), ((), ()))


def matmul(a, b):
    return jnp.dot(a, b, preferred_element_type=F32)


def vmem():
    return pl.BlockSpec(memory_space=pltpu.VMEM)


def anywhere():
    return pl.BlockSpec(memory_space=pl.ANY)


def greet(barrier, axis, me, size):
    def one(d):
        pl.semaphore_signal(
            barrier, inc=1, device_id={axis: lax.rem(me + d, size)}, device_id_type=MESH
        )

    each(1, size, one)


def each(lower, upper, body):
    def step(i, carry):
        body(i)
        return carry

    lax.fori_loop(lower, upper, step, 0)


class Place:
    def __init__(self):
        self.me = lax.axis_index("exp")
        self.x = self.me // (NZ * NY)
        self.z = lax.rem(self.me // NY, NZ)
        self.y = lax.rem(self.me, NY)

    def index(self, x, z, y):
        return (lax.rem(x, NX) * NZ + lax.rem(z, NZ)) * NY + lax.rem(y, NY)

    def plus(self, offset):
        dx, dz, dy = offset
        return self.index(self.x + dx, self.z + dz, self.y + dy)

    def minus(self, offset):
        dx, dz, dy = offset
        return self.index(self.x + NX - dx, self.z + NZ - dz, self.y + NY - dy)


class Route:
    def __init__(self, kind, first, count):
        self.kind = kind
        self.first, self.count = first, count
        self.rows = pl.ds(first, count)
        self.line = NX if kind == "x" else NZ
        self.plane = NX * NZ * NY // self.line

    def offset(self, d, g):
        if self.kind == "z":
            return (g // NY, d, lax.rem(g, NY))
        if self.kind == "y":
            return (g // NZ, lax.rem(g, NZ), d)
        return (d, g // NY, lax.rem(g, NY))

    def split(self, offset):
        dx, dz, dy = offset
        if self.kind == "z":
            return dz, dx * NY + dy
        if self.kind == "y":
            return dy, dx * NZ + dz
        return dx, dz * NY + dy


ROUTES = (Route("z", 0, 48), Route("y", 48, 48), Route("x", 96, 32))


def remote(src, dst, send, recv, peer):
    return pltpu.make_async_remote_copy(
        src_ref=src,
        dst_ref=dst,
        send_sem=send,
        recv_sem=recv,
        device_id={"exp": peer},
        device_id_type=MESH,
    )


class Reduce:
    def __init__(self, place, route, src, bufs):
        self.place, self.route, self.src = place, route, src
        self.got, self.out, self.fin, self.s1, self.r1, self.s2, self.r2 = bufs

    def first(self, d, g):
        route = self.route
        return remote(
            self.src.at[self.place.plus(route.offset(d, g)), route.rows],
            self.got.at[d - 1, g],
            self.s1.at[d - 1, g],
            self.r1.at[d - 1, g],
            self.place.plus(route.offset(d, 0)),
        )

    def second(self, g):
        return remote(
            self.out.at[g],
            self.fin.at[g],
            self.s2.at[g],
            self.r2.at[g],
            self.place.plus(self.route.offset(0, g)),
        )

    def send(self, offset):
        d, g = self.route.split(offset)

        @pl.when(d > 0)
        def _():
            self.first(d, g).start()

    def combined(self, g):
        route = self.route
        total = self.src[self.place.plus(route.offset(0, g)), route.rows].astype(F32)
        for d in range(1, route.line):
            self.first(d, g).wait_recv()
            total = total + self.got[d - 1, g].astype(F32)
        return total

    def relay(self, g):
        self.out[g] = self.combined(g).astype(BF)
        self.second(g).start()

    def add(self, g, acc_ref):
        self.second(g).wait_recv()
        acc_ref[self.route.rows] += self.fin[g].astype(F32)

    def finish(self):
        route = self.route

        def one(g):
            for d in range(1, route.line):
                self.first(d, g).wait_send()

        each(0, route.plane, one)
        each(1, route.plane, lambda g: self.second(g).wait_send())


def reduce_scratch(route, cols):
    lines, plane = route.line - 1, route.plane
    return [
        pltpu.VMEM((lines, plane, route.count, cols), BF),
        pltpu.VMEM((plane, route.count, cols), BF),
        pltpu.VMEM((plane, route.count, cols), BF),
        pltpu.SemaphoreType.DMA((lines, plane)),
        pltpu.SemaphoreType.DMA((lines, plane)),
        pltpu.SemaphoreType.DMA((plane,)),
        pltpu.SemaphoreType.DMA((plane,)),
    ]


class Gather:
    def __init__(self, place, route, whole, bufs):
        self.place, self.route, self.whole = place, route, whole
        self.s1, self.s2, self.r = bufs

    def near(self, g, source):
        block = self.whole.at[source, self.route.rows]
        return remote(
            block, block, self.s1.at[g], self.r.at[0, g], self.place.plus(self.route.offset(0, g))
        )

    def far(self, d, g, source):
        block = self.whole.at[source, self.route.rows]
        return remote(
            block,
            block,
            self.s2.at[d - 1, g],
            self.r.at[d, g],
            self.place.plus(self.route.offset(d, 0)),
        )

    def begin(self):
        each(1, self.route.plane, lambda g: self.near(g, self.place.me).start())
        self.forward(0)

    def forward(self, g):
        source = self.place.minus(self.route.offset(0, g))
        for d in range(1, self.route.line):
            self.far(d, g, source).start()

    def relay(self, g):
        self.near(g, self.place.minus(self.route.offset(0, g))).wait_recv()
        self.forward(g)

    def arrive(self, offset):
        d, g = self.route.split(offset)

        @pl.when(d > 0)
        def _():
            self.far(d, g, self.place.minus(offset)).wait_recv()

    def finish(self):
        route = self.route

        def one(g):
            source = self.place.minus(route.offset(0, g))
            for d in range(1, route.line):
                self.far(d, g, source).wait_send()

        each(0, route.plane, one)
        each(1, route.plane, lambda g: self.near(g, self.place.me).wait_send())


def gather_scratch(route):
    lines, plane = route.line - 1, route.plane
    return [
        pltpu.SemaphoreType.DMA((plane,)),
        pltpu.SemaphoreType.DMA((lines, plane)),
        pltpu.SemaphoreType.DMA((route.line, plane)),
    ]


def offset_of(o):
    return (o // (NZ * NY), lax.rem(o // NY, NZ), lax.rem(o, NY))


def spread(block, lanes):
    wide = jnp.concatenate([block] * (lanes // block.shape[1]), axis=1)
    step = lax.rem(lax.broadcasted_iota(jnp.int32, wide.shape, 1) // TOP, STEPS)
    row = lax.broadcasted_iota(jnp.int32, wide.shape, 0)
    return jnp.sum(jnp.where(step == row, wide, 0.0), 0, keepdims=True)


def attend_kernel(peers, groups, *refs):
    (
        len_ref,
        q_ref,
        nk_ref,
        cache_ref,
        wv_ref,
        wo_ref,
        res_ref,
        gain_ref,
        ids_ref,
        gates_ref,
        xall_ref,
        att_ref,
        meta_ref,
        cache_v,
        wo_s,
        res_s,
        q_s,
        nk_s,
        new_s,
        ctx_s,
        send_v,
        acc,
        ssq_s,
        ssq_r,
        nrm_v,
        meta_v,
        cache_sem,
        ssq_send,
        ssq_recv,
        meta_send,
        meta_recv,
        f_send,
        f_recv,
        m_send,
        m_recv,
        own_sem,
    ) = refs[:36]
    place = Place()
    me = place.me
    fs = lax.axis_index("fsdp")
    tokens = q_s.shape[0]
    latent = wv_ref.shape[0]
    width = wo_ref.shape[1] // peers
    barrier = pltpu.get_barrier_semaphore()
    greet(barrier, "exp", me, peers)
    greet(barrier, "fsdp", fs, groups)
    sums = [Reduce(place, r, send_v, refs[36 + 7 * i : 43 + 7 * i]) for i, r in enumerate(ROUTES)]

    def cache_copy(i):
        rows = pl.ds(ROUTES[i].first // STEPS, ROUTES[i].count // STEPS)
        return pltpu.make_async_copy(cache_ref.at[rows], cache_v.at[rows], cache_sem.at[i])

    for i in range(len(ROUTES)):
        cache_copy(i).start()

    lane = lax.broadcasted_iota(jnp.int32, (1, 128), 1)
    here = lane // (STEPS * TOP) == lax.rem(me, 4)
    own_ids = jnp.where(here, spread(ids_ref[0].astype(F32), 128), 0.0)
    own_gates = jnp.where(here, spread(gates_ref[0], 128), 0.0)
    meta_v[me] = jnp.concatenate([own_ids, own_gates, jnp.zeros((6, 128), F32)], axis=0)

    def meta_copy(d, slot):
        return remote(
            meta_v.at[slot],
            meta_v.at[slot],
            meta_send.at[d],
            meta_recv.at[slot],
            lax.rem(me + d, peers),
        )

    for b in range(tokens // 16):
        rows = slice(b * 16, b * 16 + 16)
        q_s[rows, :] = jnp.concatenate(
            [q_ref[4 * b + i].astype(F32) for i in range(4)], axis=0
        ).astype(BF)
        nk_s[rows, :] = jnp.concatenate(
            [nk_ref[4 * b + i].astype(F32) for i in range(4)], axis=0
        ).astype(BF)

    gain = jnp.zeros((1, width), F32)
    pad = jnp.zeros((wo_ref.shape[0], WIDE - width), BF)
    res_pad = jnp.zeros((16, WIDE - width), F32)
    for j in range(peers):
        part = slice(j * width, (j + 1) * width)
        wo_s[j] = jnp.concatenate([wo_ref[:, part], pad], axis=1)
        res = jnp.concatenate([res_ref[0, :, part].astype(F32)] * 4, axis=0)
        res_s[j] = jnp.concatenate([res, res_pad], axis=1)
        gain = jnp.where(me == j, gain_ref[:, part], gain)
    gain = jnp.concatenate([gain, jnp.zeros((1, WIDE - width), F32)], axis=1)

    token_r = lax.broadcasted_iota(jnp.int32, (tokens, tokens), 0)
    token_c = lax.broadcasted_iota(jnp.int32, (tokens, tokens), 1)
    same = (token_r // STEPS == token_c // STEPS) & (token_c <= token_r)
    fresh = lax.dot_general(q_s[...], nk_s[...], NT, preferred_element_type=F32)
    new_s[...] = jnp.where(same, fresh * score_scale, -1e30)

    pl.semaphore_wait(barrier, peers - 1 + groups - 1)
    each(1, peers, lambda d: meta_copy(d, me).start())

    which = lax.broadcasted_iota(jnp.int32, (16, 1), 0) // STEPS
    position = lax.broadcasted_iota(jnp.int32, (16, cache_ref.shape[2]), 1)

    for i, route in enumerate(ROUTES):
        cache_copy(i).wait()

        def block(b, route=route):
            rows = pl.ds(pl.multiple_of(b * 16, 16), 16)
            first = b * 4
            q16 = q_s[rows, :]
            scores = matmul(q16, cache_v[first])
            length = jnp.full(position.shape, len_ref[first])
            for n in range(1, 4):
                scores = jnp.where(which == n, matmul(q16, cache_v[first + n]), scores)
                length = jnp.where(which == n, len_ref[first + n], length)
            scores = jnp.where(position < length, scores * score_scale, -1e30)
            new = new_s[rows, :]
            highest = jnp.maximum(
                jnp.max(scores, -1, keepdims=True), jnp.max(new, -1, keepdims=True)
            )
            cache_exp = jnp.exp(scores - highest)
            new_exp = jnp.exp(new - highest)
            total = jnp.sum(cache_exp, -1, keepdims=True) + jnp.sum(new_exp, -1, keepdims=True)
            cache_w = (cache_exp / total).astype(BF)
            new_w = (new_exp / total).astype(BF)
            context = lax.dot_general(
                cache_w, cache_v[first, :latent, :], NT, preferred_element_type=F32
            )
            for n in range(1, 4):
                part = lax.dot_general(
                    cache_w, cache_v[first + n, :latent, :], NT, preferred_element_type=F32
                )
                context = jnp.where(which == n, part, context)
            context = context + matmul(new_w, nk_s[:, :latent])
            ctx_s[rows, :] = context.astype(BF)

        each(route.first // 16, (route.first + route.count) // 16, block)
        values = matmul(ctx_s[route.rows, :], wv_ref[...]).astype(BF)
        owner = (route.first + lax.broadcasted_iota(jnp.int32, (route.count, 1), 0)) // STEPS

        def project(o, route=route, values=values, owner=owner, i=i):
            offset = offset_of(o)
            j = place.plus(offset)
            part = matmul(values, wo_s[j])
            res = jnp.concatenate([res_s[j]] * (route.count // 16), axis=0)
            send_v[j, route.rows, :] = (part + jnp.where(owner == me, res, 0.0)).astype(BF)
            sums[i].send(offset)

        each(0, peers, project)

    each(1, peers, lambda d: meta_copy(d, lax.rem(me + d, peers)).wait_recv())
    whole = pltpu.make_async_copy(meta_v, meta_ref.at[fs], own_sem.at[0])
    whole.start()

    def group_copy(d, slot, src, dst, sends, recvs):
        return pltpu.make_async_remote_copy(
            src_ref=src,
            dst_ref=dst.at[slot],
            send_sem=sends.at[d],
            recv_sem=recvs.at[slot],
            device_id={"fsdp": lax.rem(fs + d, groups)},
            device_id_type=MESH,
        )

    meta_group = functools.partial(group_copy, src=meta_v, dst=meta_ref, sends=m_send, recvs=m_recv)
    for d in range(1, groups):
        meta_group(d, fs).start()

    for s in sums:
        each(1, s.route.plane, s.relay)
        acc[s.route.rows] = s.combined(0)
    for s in sums:
        each(1, s.route.plane, lambda g, s=s: s.add(g, acc))

    attended = acc[...]
    att_ref[...] = attended
    diagonal = token_r == token_c
    column = jnp.sum(attended * attended, -1, keepdims=True)
    row = jnp.sum(jnp.where(diagonal, column, 0.0), 0, keepdims=True)
    ssq_s[...] = jnp.broadcast_to(row, ssq_s.shape)

    def ssq_copy(d, slot):
        return remote(
            ssq_s, ssq_r.at[slot], ssq_send.at[d], ssq_recv.at[slot], lax.rem(me + d, peers)
        )

    each(1, peers, lambda d: ssq_copy(d, me).start())

    def add_ssq(d, total):
        slot = lax.rem(me + d, peers)
        ssq_copy(d, slot).wait_recv()
        return total + ssq_r[slot]

    total = lax.fori_loop(1, peers, add_ssq, ssq_s[...])[:1, :]
    column = jnp.sum(jnp.where(diagonal, total, 0.0), 1, keepdims=True)
    scale = lax.rsqrt(column / (width * peers) + 1e-06)
    nrm_v[...] = (attended * scale * gain).astype(BF)

    own = pltpu.make_async_copy(nrm_v, xall_ref.at[fs], own_sem.at[1])
    own.start()
    x_group = functools.partial(group_copy, src=nrm_v, dst=xall_ref, sends=f_send, recvs=f_recv)
    for d in range(1, groups):
        x_group(d, fs).start()
    for s in sums:
        s.finish()

    def close(d):
        ssq_copy(d, me).wait_send()
        meta_copy(d, me).wait_send()

    each(1, peers, close)
    for d in range(1, groups):
        meta_group(d, lax.rem(fs + d, groups)).wait_recv()
        x_group(d, lax.rem(fs + d, groups)).wait_recv()
    for d in range(1, groups):
        meta_group(d, fs).wait_send()
        x_group(d, fs).wait_send()
    whole.wait()
    own.wait()


def attend(lens, q, nk, cache, wv, wo, res, gain, ids, gates, peers, groups):
    tokens = q.shape[0] * q.shape[1]
    key = q.shape[2]
    scratch = [
        pltpu.VMEM(cache.shape, BF),
        pltpu.VMEM((peers, wo.shape[0], WIDE), BF),
        pltpu.VMEM((peers, 16, WIDE), F32),
        pltpu.VMEM((tokens, key), BF),
        pltpu.VMEM((tokens, key), BF),
        pltpu.VMEM((tokens, tokens), F32),
        pltpu.VMEM((tokens, wv.shape[0]), BF),
        pltpu.VMEM((peers, tokens, WIDE), BF),
        pltpu.VMEM((tokens, WIDE), F32),
        pltpu.VMEM((8, tokens), F32),
        pltpu.VMEM((peers, 8, tokens), F32),
        pltpu.VMEM((tokens, WIDE), BF),
        pltpu.VMEM((peers, 8, 128), F32),
        pltpu.SemaphoreType.DMA((len(ROUTES),)),
        pltpu.SemaphoreType.DMA((peers,)),
        pltpu.SemaphoreType.DMA((peers,)),
        pltpu.SemaphoreType.DMA((peers,)),
        pltpu.SemaphoreType.DMA((peers,)),
        pltpu.SemaphoreType.DMA((groups,)),
        pltpu.SemaphoreType.DMA((groups,)),
        pltpu.SemaphoreType.DMA((groups,)),
        pltpu.SemaphoreType.DMA((groups,)),
        pltpu.SemaphoreType.DMA((2,)),
    ]
    for route in ROUTES:
        scratch += reduce_scratch(route, WIDE)
    return pl.pallas_call(
        functools.partial(attend_kernel, peers, groups),
        out_shape=(
            jax.ShapeDtypeStruct((groups, tokens, WIDE), BF),
            jax.ShapeDtypeStruct((tokens, WIDE), F32),
            jax.ShapeDtypeStruct((groups, peers, 8, 128), F32),
        ),
        in_specs=[pl.BlockSpec(memory_space=pltpu.SMEM)] + [vmem()] * 2 + [anywhere()] + [vmem()] * 6,
        out_specs=(anywhere(), vmem(), anywhere()),
        scratch_shapes=scratch,
        compiler_params=pltpu.CompilerParams(
            collective_id=0, has_side_effects=True, vmem_limit_bytes=HIGH
        ),
        name="attend",
    )(lens, q, nk, cache, wv, wo, res, gain, ids, gates)


def experts_kernel(peers, groups, *refs):
    (
        x_ref,
        meta_ref,
        att_ref,
        wg_ref,
        wu_ref,
        wd_ref,
        out_ref,
        wg_v,
        wu_v,
        wd_v,
        dense,
        part_v,
        acc,
        hid_v,
        code_s,
        gate_s,
        routed_v,
        routed_r,
        send_v,
        recv_v,
        w_sem,
        f_send,
        f_recv,
        o_send,
        o_recv,
    ) = refs[:25]
    place = Place()
    me = place.me
    fs = lax.axis_index("fsdp")
    experts, depth, half = wg_ref.shape
    tokens = x_ref.shape[0]
    rows = part_v.shape[1]
    block = tokens // peers
    own_rows = send_v.shape[1]
    barrier = pltpu.get_barrier_semaphore()
    greet(barrier, "exp", me, peers)
    greet(barrier, "fsdp", fs, groups)
    rest = refs[25:]
    sums = [Reduce(place, r, part_v, rest[7 * i : 7 * i + 7]) for i, r in enumerate(ROUTES)]
    rest = rest[7 * len(ROUTES) :]
    gathers = [Gather(place, r, hid_v, rest[3 * i : 3 * i + 3]) for i, r in enumerate(ROUTES)]

    def weight_copy(n, e):
        src = (wg_ref, wu_ref, wd_ref)[n]
        dst = (wg_v, wu_v, wd_v)[n]
        return pltpu.make_async_copy(src.at[e], dst.at[e], w_sem.at[n, e])

    def load(e):
        weight_copy(0, e).start()
        weight_copy(1, e).start()

    each(0, experts, load)
    each(0, experts, lambda e: weight_copy(2, e).start())

    lane = lax.broadcasted_iota(jnp.int32, (1, rows), 1)

    def read_meta(j):
        info = meta_ref[4 * j] + meta_ref[4 * j + 1] + meta_ref[4 * j + 2] + meta_ref[4 * j + 3]
        code_s[j] = info[0:1, :].astype(jnp.int32) * block + lane // TOP
        gate_s[j] = info[1:2, :]

    each(0, peers, read_meta)

    def multiply(e):
        weight_copy(0, e).wait()
        weight_copy(1, e).wait()
        x = x_ref[...][:, :depth]
        spot = pl.ds(pl.multiple_of(e * block, block), block)
        gate = matmul(x, wg_v[e]).astype(BF)
        dense[:, spot, :half] = gate.reshape(peers, block, half)
        up = matmul(x, wu_v[e]).astype(BF)
        dense[:, spot, half:] = up.reshape(peers, block, half)

    each(0, experts, multiply)
    pl.semaphore_wait(barrier, peers - 1 + groups - 1)

    diagonal = lax.broadcasted_iota(jnp.int32, (rows, rows), 0) == lax.broadcasted_iota(
        jnp.int32, (rows, rows), 1
    )
    slot_c = lax.broadcasted_iota(jnp.int32, (rows, experts * block), 1)
    slot_r = lax.broadcasted_iota(jnp.int32, (experts * block, rows), 0)

    def pick(o):
        offset = offset_of(o)
        j = place.plus(offset)
        code = jnp.sum(jnp.where(diagonal, code_s[j], 0), 1, keepdims=True)
        chosen = (code == slot_c).astype(F32).astype(BF)
        part_v[j] = matmul(chosen, dense[j]).astype(BF)
        for s in sums:
            s.send(offset)

    each(0, peers, pick)

    for s in sums:
        each(1, s.route.plane, s.relay)
        acc[s.route.rows] = s.combined(0)
    for s in sums:
        each(1, s.route.plane, lambda g, s=s: s.add(g, acc))

    gate = acc[:, :half]
    weight = jnp.sum(jnp.where(diagonal, gate_s[me], 0.0), 1, keepdims=True)
    hid_v[me] = (gate / (1.0 + jnp.exp(-gate)) * acc[:, half:] * weight).astype(BF)

    for g in gathers:
        g.begin()
    for g in gathers:
        each(1, g.route.plane, g.relay)

    def expand(o):
        offset = offset_of(o)
        j = place.minus(offset)
        for g in gathers:
            g.arrive(offset)
        chosen = (code_s[j] == slot_r).astype(F32).astype(BF)
        full = matmul(chosen, hid_v[j]).astype(BF)
        spot = pl.ds(pl.multiple_of(j * block, block), block)
        dense[:, spot, :half] = full.reshape(experts, block, half)

    each(0, peers, expand)
    each(0, experts, lambda e: weight_copy(2, e).wait())

    def group_copy(d, slot):
        peer = lax.rem(fs + d, groups)
        return pltpu.make_async_remote_copy(
            src_ref=routed_v.at[peer],
            dst_ref=routed_r.at[slot],
            send_sem=f_send.at[d],
            recv_sem=f_recv.at[slot],
            device_id={"fsdp": peer},
            device_id_type=MESH,
        )

    def shares(piece):
        spot = pl.ds(pl.multiple_of(piece * (tokens // groups), 128), tokens // groups)

        def one(e, total):
            return total + lax.dot_general(
                dense[e, spot, :half], wd_v[e], NT, preferred_element_type=F32
            )

        return lax.fori_loop(0, experts, one, jnp.zeros((tokens // groups, depth), F32))

    for d in range(1, groups):
        peer = lax.rem(fs + d, groups)
        routed_v[peer, :, :depth] = shares(peer).astype(BF)
        group_copy(d, fs).start()
    mixed = att_ref[:, :depth] + shares(fs)
    for d in range(1, groups):
        slot = lax.rem(fs + d, groups)
        group_copy(d, slot).wait_recv()
        mixed = mixed + routed_r[slot][:, :depth].astype(F32)
    for j in range(peers):
        send_v[j, :, :depth] = mixed[j * own_rows : (j + 1) * own_rows, :]

    def out_copy(d, slot):
        peer = lax.rem(me + d, peers)
        return remote(send_v.at[peer], recv_v.at[slot], o_send.at[d], o_recv.at[slot], peer)

    each(1, peers, lambda d: out_copy(d, me).start())
    recv_v[me] = send_v[me]
    for s in sums:
        s.finish()
    for g in gathers:
        g.finish()
    for d in range(1, groups):
        group_copy(d, fs).wait_send()
    each(1, peers, lambda d: out_copy(d, lax.rem(me + d, peers)).wait_recv())
    for j in range(peers):
        out_ref[0, :, j * depth : (j + 1) * depth] = recv_v[j][:, :depth]
    each(1, peers, lambda d: out_copy(d, me).wait_send())


def expert_layer(x, meta, att, wg, wu, wd, peers, groups):
    tokens = x.shape[0]
    experts, depth, half = wg.shape
    block = tokens // peers
    rows = block * TOP
    own = att.shape[0] // peers
    scratch = [
        pltpu.VMEM(wg.shape, BF),
        pltpu.VMEM(wg.shape, BF),
        pltpu.VMEM(wg.shape, BF),
        pltpu.VMEM((peers, experts * block, 2 * half), BF),
        pltpu.VMEM((peers, rows, 2 * half), BF),
        pltpu.VMEM((rows, 2 * half), F32),
        pltpu.VMEM((peers, rows, half), BF),
        pltpu.VMEM((peers, 1, rows), jnp.int32),
        pltpu.VMEM((peers, 1, rows), F32),
        pltpu.VMEM((groups, tokens // groups, WIDE), BF),
        pltpu.VMEM((groups, tokens // groups, WIDE), BF),
        pltpu.VMEM((peers, own, WIDE), F32),
        pltpu.VMEM((peers, own, WIDE), F32),
        pltpu.SemaphoreType.DMA((3, experts)),
        pltpu.SemaphoreType.DMA((groups,)),
        pltpu.SemaphoreType.DMA((groups,)),
        pltpu.SemaphoreType.DMA((peers,)),
        pltpu.SemaphoreType.DMA((peers,)),
    ]
    for route in ROUTES:
        scratch += reduce_scratch(route, 2 * half)
    for route in ROUTES:
        scratch += gather_scratch(route)
    return pl.pallas_call(
        functools.partial(experts_kernel, peers, groups),
        out_shape=jax.ShapeDtypeStruct((1, own, depth * peers), F32),
        in_specs=[vmem()] * 3 + [anywhere()] * 3,
        out_specs=vmem(),
        scratch_shapes=scratch,
        compiler_params=pltpu.CompilerParams(
            collective_id=1, has_side_effects=True, vmem_limit_bytes=HIGH
        ),
        name="experts",
    )(x, meta, att, wg, wu, wd)


def shards(
    residual,
    gain,
    queries,
    new_keys,
    cache,
    lengths,
    w_value,
    w_out,
    w_gate,
    w_up,
    w_down,
    expert_ids,
    gates,
):
    peers = lax.axis_size("exp")
    groups = lax.axis_size("fsdp")
    xall, att, meta = attend(
        lengths,
        queries[:, :, 0, :],
        new_keys,
        cache,
        w_value[0],
        w_out[0],
        residual,
        gain.reshape(1, -1),
        expert_ids,
        gates,
        peers,
        groups,
    )
    x = xall.reshape(-1, WIDE)
    meta = meta.reshape(groups * peers, 8, 128)
    return expert_layer(x, meta, att, w_gate, w_up, w_down, peers, groups)


def solution(mesh):
    return jax.shard_map(
        shards,
        mesh=mesh,
        in_specs=(
            P(("fsdp", "exp"), None, None),
            P(),
            P("fsdp", None, "exp", None),
            P("fsdp", None, None),
            P("fsdp", None, None),
            P("fsdp"),
            P("exp", None, None),
            P("exp", None, None),
            P(None, "exp", "fsdp"),
            P(None, "exp", "fsdp"),
            P(None, "exp", "fsdp"),
            P(("fsdp", "exp"), None, None),
            P(("fsdp", "exp"), None, None),
        ),
        out_specs=P(("fsdp", "exp"), None, None),
        check_vma=False,
    )
```

time: 635 us -> 167 us (0.26)
  waiting for transfers between devices: 388 us -> 0 us
  Pallas kernels: 0 us -> 164 us
  blocking collectives: 136 us -> 0 us
  matrix products: 32.9 us -> 0 us
  starting transfers between devices: 29.1 us -> 0 us
  local copies, waits for them, and re-layouts: 23.6 us -> 1.55 us
  between operations: 14.3 us -> 0.02 us
  other arithmetic: 10.1 us -> 0 us
    unnamed x2 -> x0, waiting for transfers between devices: 320 us -> none
    pallas_call x0 -> x2, Pallas kernels: none -> 164 us  [the longest x1 102 us: expert_layer(): pl.pallas_call(functools.partial(experts_kernel, peers, groups), out_shap...]
    all_to_all x2 -> x0, blocking collectives: 136 us -> none  [the longest x1 77 us: shards(): lax.all_to_all(copies, ('exp', 'fsdp'), split_axis=0, concat_axis=0, tile...]
    all_to_all x3 -> x0, waiting for transfers between devices: 68.9 us -> none  [the longest x1 35 us: shards(): lax.all_to_all(w_up, 'exp', split_axis=0, concat_axis=1, tiled=True)]
    dot_general x10 -> x0, matrix products: 32.9 us -> none  [the longest x1 10.1 us: expert_share(): jnp.einsum('mf,df->md', hidden, down_mat, preferred_element_type=jnp.floa...]
    all_to_all x3 -> x0, starting transfers between devices: 29 us -> none  [the longest x1 11.6 us: shards(): lax.all_to_all(w_down, 'exp', split_axis=0, concat_axis=1, tiled=True)]
    all_to_all x2 -> x0, local copies, waits for them, and re-layouts: 16.5 us -> none  [the longest x1 8.41 us: shards(): lax.all_to_all(copies, ('exp', 'fsdp'), split_axis=0, concat_axis=0, tile...]
    reduce_sum x6 -> x0, other arithmetic: 9.64 us -> none  [the longest x1 7.96 us: shards(): jnp.sum(returned.reshape(experts, groups, capacity, width).astype(jnp.flo...]
  transfers between devices with their start and end apart: 4 -> 0, of which waited for: 3 -> 0; matrix products, arithmetic and copies ran while one was open for 4% -> 0% of each run, Pallas kernels for 0% -> 0%
where the time goes in v2:
time: 167 us; the launch traced here: 165 us
  Pallas kernels  164 us (98%)
    pallas_call x1, Pallas kernels, expert_layer(): pl.pallas_call(functools.partial(experts_kernel, peers, groups), out_shap...  102 us
    pallas_call x1, Pallas kernels, attend(): pl.pallas_call(functools.partial(attend_kernel, peers, groups), out_shape...  62.3 us

profile of v2, /device:TPU:1, one launch (start us, length us, event | category | flops | bytes accessed | tf_op | source)
XLA Modules:
  0.0 165.4 jit_solution(6051110608007848199)
XLA Ops:
  0.0 62.3 %attend.1 = (bf16[4,128,256]{2,1,0:T(8,128)(2,1)}, f32[128,256]{1,0:T(8,128)}, f32[4,32,8,128]{3,2,1,0:T(8,128)}) custom-call(s32[32]{0:T(128)} %refs_0_.1, bf16[32,4,576]{2,1,0:T(4,128)(2,1)} %bitcast.9, bf16[32,4,576]{2,1,0:T(4,128)(2,1)} %refs_2_.1, bf16[32,576,256]{2,1,0:T(8,128)(2,1)} %refs_3_.2, bf16[512,128]{1,0:T(8,128)(2,1)} %bitcast.10, ...), custom_call_target="tpu_custom_call" | custom-call | tf_op jit(solution)/shard_map/attend/pallas_call | solution.py:504
  62.3 101.5 %experts.1 = f32[1,4,7168]{2,1,0:T(4,128)} custom-call(bf16[512,256]{1,0:T(8,128)(2,1)} %bitcast.8, f32[128,8,128]{2,1,0:T(8,128)} %bitcast.7, f32[128,256]{1,0:T(8,128)} %get-tuple-element.10.refs_2_, bf16[32,224,256]{2,1,0:T(8,128)(2,1)} %refs_3_.3, bf16[32,224,256]{2,1,0:T(8,128)(2,1)} %refs_4_.1, bf16[32,224,256]{2,1,0:T(8,128)(2,1)} %refs_5_.1), custom_call_target="tpu_custom_call" | custom-call | tf_op jit(solution)/shard_map/experts/pallas_call | solution.py:725
  163.8 1.6 copy.15

commit v3 on v2

v3 whole, which is shorter than its diff:
```python
import functools

import jax
import jax.numpy as jnp
from jax import lax
from jax.experimental import pallas as pl
from jax.experimental.pallas import tpu as pltpu
from jax.sharding import PartitionSpec as P

TOP = 8
STEPS = 4
score_scale = 0.07216878364870322
MESH = pl.DeviceIdType.MESH
BF = jnp.bfloat16
F32 = jnp.float32
WIDE = 256
HIGH = 58 * 1024 * 1024
NX, NZ, NY = 2, 4, 4
NT = (((1,), (1,)), ((), ()))


def matmul(a, b):
    return jnp.dot(a, b, preferred_element_type=F32)


def vmem():
    return pl.BlockSpec(memory_space=pltpu.VMEM)


def anywhere():
    return pl.BlockSpec(memory_space=pl.ANY)


def greet(barrier, axis, me, size):
    def one(d):
        pl.semaphore_signal(
            barrier, inc=1, device_id={axis: lax.rem(me + d, size)}, device_id_type=MESH
        )

    each(1, size, one)


def each(lower, upper, body):
    def step(i, carry):
        body(i)
        return carry

    lax.fori_loop(lower, upper, step, 0)


class Place:
    def __init__(self):
        self.me = lax.axis_index("exp")
        self.x = self.me // (NZ * NY)
        self.z = lax.rem(self.me // NY, NZ)
        self.y = lax.rem(self.me, NY)

    def index(self, x, z, y):
        return (lax.rem(x, NX) * NZ + lax.rem(z, NZ)) * NY + lax.rem(y, NY)

    def plus(self, offset):
        dx, dz, dy = offset
        return self.index(self.x + dx, self.z + dz, self.y + dy)

    def minus(self, offset):
        dx, dz, dy = offset
        return self.index(self.x + NX - dx, self.z + NZ - dz, self.y + NY - dy)


class Route:
    def __init__(self, kind, first, count):
        self.kind = kind
        self.first, self.count = first, count
        self.rows = pl.ds(first, count)
        self.line = NX if kind == "x" else NZ
        self.plane = NX * NZ * NY // self.line

    def offset(self, d, g):
        if self.kind == "z":
            return (g // NY, d, lax.rem(g, NY))
        if self.kind == "y":
            return (g // NZ, lax.rem(g, NZ), d)
        return (d, g // NY, lax.rem(g, NY))

    def split(self, offset):
        dx, dz, dy = offset
        if self.kind == "z":
            return dz, dx * NY + dy
        if self.kind == "y":
            return dy, dx * NZ + dz
        return dx, dz * NY + dy


ROUTES = (Route("z", 0, 48), Route("y", 48, 48), Route("x", 96, 32))


def remote(src, dst, send, recv, peer):
    return pltpu.make_async_remote_copy(
        src_ref=src,
        dst_ref=dst,
        send_sem=send,
        recv_sem=recv,
        device_id={"exp": peer},
        device_id_type=MESH,
    )


class Reduce:
    def __init__(self, place, route, src, bufs):
        self.place, self.route, self.src = place, route, src
        self.got, self.out, self.fin, self.s1, self.r1, self.s2, self.r2 = bufs

    def first(self, d, g):
        route = self.route
        return remote(
            self.src.at[self.place.plus(route.offset(d, g)), route.rows],
            self.got.at[d - 1, g],
            self.s1.at[d - 1, g],
            self.r1.at[d - 1, g],
            self.place.plus(route.offset(d, 0)),
        )

    def second(self, g):
        return remote(
            self.out.at[g],
            self.fin.at[g],
            self.s2.at[g],
            self.r2.at[g],
            self.place.plus(self.route.offset(0, g)),
        )

    def send(self, offset):
        d, g = self.route.split(offset)

        @pl.when(d > 0)
        def _():
            self.first(d, g).start()

    def combined(self, g):
        route = self.route
        total = self.src[self.place.plus(route.offset(0, g)), route.rows].astype(F32)
        for d in range(1, route.line):
            self.first(d, g).wait_recv()
            total = total + self.got[d - 1, g].astype(F32)
        return total

    def add(self, g, acc_ref):
        self.second(g).wait_recv()
        acc_ref[self.route.rows] += self.fin[g].astype(F32)

    def step(self, g, acc_ref):
        total = self.combined(g)

        @pl.when(g == 0)
        def _():
            acc_ref[self.route.rows] = total

        @pl.when(g != 0)
        def _():
            self.out[g] = total.astype(BF)
            self.second(g).start()

    def finish(self):
        route = self.route

        def one(g):
            for d in range(1, route.line):
                self.first(d, g).wait_send()

        each(0, route.plane, one)
        each(1, route.plane, lambda g: self.second(g).wait_send())


def reduce_scratch(route, cols):
    lines, plane = route.line - 1, route.plane
    return [
        pltpu.VMEM((lines, plane, route.count, cols), BF),
        pltpu.VMEM((plane, route.count, cols), BF),
        pltpu.VMEM((plane, route.count, cols), BF),
        pltpu.SemaphoreType.DMA((lines, plane)),
        pltpu.SemaphoreType.DMA((lines, plane)),
        pltpu.SemaphoreType.DMA((plane,)),
        pltpu.SemaphoreType.DMA((plane,)),
    ]


class Gather:
    def __init__(self, place, route, whole, bufs):
        self.place, self.route, self.whole = place, route, whole
        self.s1, self.s2, self.r = bufs

    def near(self, g, source):
        block = self.whole.at[source, self.route.rows]
        return remote(
            block, block, self.s1.at[g], self.r.at[0, g], self.place.plus(self.route.offset(0, g))
        )

    def far(self, d, g, source):
        block = self.whole.at[source, self.route.rows]
        return remote(
            block,
            block,
            self.s2.at[d - 1, g],
            self.r.at[d, g],
            self.place.plus(self.route.offset(d, 0)),
        )

    def begin(self):
        each(1, self.route.plane, lambda g: self.near(g, self.place.me).start())
        self.forward(0)

    def forward(self, g):
        source = self.place.minus(self.route.offset(0, g))
        for d in range(1, self.route.line):
            self.far(d, g, source).start()

    def relay(self, g):
        self.near(g, self.place.minus(self.route.offset(0, g))).wait_recv()
        self.forward(g)

    def arrive(self, offset):
        d, g = self.route.split(offset)

        @pl.when(d > 0)
        def _():
            self.far(d, g, self.place.minus(offset)).wait_recv()

    def finish(self):
        route = self.route

        def one(g):
            source = self.place.minus(route.offset(0, g))
            for d in range(1, route.line):
                self.far(d, g, source).wait_send()

        each(0, route.plane, one)
        each(1, route.plane, lambda g: self.near(g, self.place.me).wait_send())


def gather_scratch(route):
    lines, plane = route.line - 1, route.plane
    return [
        pltpu.SemaphoreType.DMA((plane,)),
        pltpu.SemaphoreType.DMA((lines, plane)),
        pltpu.SemaphoreType.DMA((route.line, plane)),
    ]


def offset_of(o):
    return (o // (NZ * NY), lax.rem(o // NY, NZ), lax.rem(o, NY))


def spread(block, lanes):
    wide = jnp.concatenate([block] * (lanes // block.shape[1]), axis=1)
    step = lax.rem(lax.broadcasted_iota(jnp.int32, wide.shape, 1) // TOP, STEPS)
    row = lax.broadcasted_iota(jnp.int32, wide.shape, 0)
    return jnp.sum(jnp.where(step == row, wide, 0.0), 0, keepdims=True)


def layer_kernel(peers, groups, *refs):
    (
        len_ref,
        q_ref,
        nk_ref,
        cache_ref,
        wv_ref,
        wo_ref,
        res_ref,
        gain_ref,
        ids_ref,
        gates_ref,
        wg_ref,
        wu_ref,
        wd_ref,
        out_ref,
        dense,
        wo_v,
        wo_s,
        res_s,
        q_s,
        nk_s,
        new_s,
        ctx_s,
        send_v,
        att,
        ssq_s,
        ssq_r,
        sum_v,
        x_v,
        meta_v,
        wg_v,
        wu_v,
        wd_v,
        part_v,
        acc,
        hid_v,
        code_s,
        gate_s,
        routed_v,
        routed_r,
        home_s,
        home_r,
        cache_sem,
        wo_sem,
        w_sem,
        ssq_send,
        ssq_recv,
        meta_send,
        meta_recv,
        g_send,
        g_recv,
        o_send,
        o_recv,
    ) = refs[:52]
    place = Place()
    me = place.me
    fs = lax.axis_index("fsdp")
    tokens = q_s.shape[0]
    latent = wv_ref.shape[0]
    experts, depth, half = wg_ref.shape
    rows = part_v.shape[1]
    block = rows // TOP
    per = peers // groups
    own_rows = home_s.shape[1]
    barrier = pltpu.get_barrier_semaphore()
    rest = refs[52:]
    heads = [Reduce(place, r, send_v, rest[7 * i : 7 * i + 7]) for i, r in enumerate(ROUTES)]
    rest = rest[7 * len(ROUTES) :]
    sums = [Reduce(place, r, part_v, rest[7 * i : 7 * i + 7]) for i, r in enumerate(ROUTES)]
    rest = rest[7 * len(ROUTES) :]
    gathers = [Gather(place, r, hid_v, rest[3 * i : 3 * i + 3]) for i, r in enumerate(ROUTES)]

    def group_copy(n, d, block_ref):
        return pltpu.make_async_remote_copy(
            src_ref=block_ref,
            dst_ref=block_ref,
            send_sem=g_send.at[n, d],
            recv_sem=g_recv.at[n, d],
            device_id={"fsdp": lax.rem(fs + d, groups)},
            device_id_type=MESH,
        )

    def from_group(d):
        return lax.rem(fs + groups - d, groups)

    def cache_copy(i, n):
        span = pl.ds(ROUTES[i].first // STEPS, ROUTES[i].count // STEPS)
        positions = cache_ref.shape[2]
        if n == 0:
            src = cache_ref.at[span, pl.ds(0, latent)]
            dst = dense.at[span, pl.ds(0, latent), pl.ds(0, positions)]
        else:
            left = cache_ref.shape[1] - latent
            src = cache_ref.at[span, pl.ds(latent, left)]
            dst = dense.at[span, pl.ds(0, left), pl.ds(positions, positions)]
        return pltpu.make_async_copy(src, dst, cache_sem.at[i, n])

    def weight_copy(n, e):
        src = (wg_ref, wu_ref, wd_ref)[n]
        dst = (wg_v, wu_v, wd_v)[n]
        return pltpu.make_async_copy(src.at[e], dst.at[e], w_sem.at[n, e])

    out_copy = pltpu.make_async_copy(wo_ref, wo_v, wo_sem)
    for n in range(2):
        cache_copy(0, n).start()
    out_copy.start()
    for i in range(1, len(ROUTES)):
        for n in range(2):
            cache_copy(i, n).start()
    greet(barrier, "exp", me, peers)
    greet(barrier, "fsdp", fs, groups)

    for b in range(tokens // 16):
        span = slice(b * 16, b * 16 + 16)
        q_s[span, :] = jnp.concatenate(
            [q_ref[4 * b + i].astype(F32) for i in range(4)], axis=0
        ).astype(BF)
        nk_s[span, :] = jnp.concatenate(
            [nk_ref[4 * b + i].astype(F32) for i in range(4)], axis=0
        ).astype(BF)

    token_r = lax.broadcasted_iota(jnp.int32, (tokens, tokens), 0)
    token_c = lax.broadcasted_iota(jnp.int32, (tokens, tokens), 1)
    diagonal = token_r == token_c
    same = (token_r // STEPS == token_c // STEPS) & (token_c <= token_r)
    fresh = lax.dot_general(q_s[...], nk_s[...], NT, preferred_element_type=F32)
    new_s[...] = jnp.where(same, fresh * score_scale, -1e30)

    which = lax.broadcasted_iota(jnp.int32, (16, 1), 0) // STEPS
    position = lax.broadcasted_iota(jnp.int32, (16, cache_ref.shape[2]), 1)
    rope = cache_ref.shape[1] - latent

    def attend(b):
        span = pl.ds(pl.multiple_of(b * 16, 16), 16)
        first = b * 4
        q16 = q_s[span, :]

        def score(row):
            return matmul(q16[:, :latent], dense[row, :, : position.shape[1]]) + matmul(
                q16[:, latent:], dense[row, :rope, position.shape[1] :]
            )

        scores = score(first)
        length = jnp.full(position.shape, len_ref[first])
        for n in range(1, 4):
            scores = jnp.where(which == n, score(first + n), scores)
            length = jnp.where(which == n, len_ref[first + n], length)
        scores = jnp.where(position < length, scores * score_scale, -1e30)
        new = new_s[span, :]
        highest = jnp.maximum(jnp.max(scores, -1, keepdims=True), jnp.max(new, -1, keepdims=True))
        cache_exp = jnp.exp(scores - highest)
        new_exp = jnp.exp(new - highest)
        total = jnp.sum(cache_exp, -1, keepdims=True) + jnp.sum(new_exp, -1, keepdims=True)
        cache_w = (cache_exp / total).astype(BF)
        new_w = (new_exp / total).astype(BF)

        def mix(row):
            return lax.dot_general(
                cache_w, dense[row, :, : position.shape[1]], NT, preferred_element_type=F32
            )

        context = mix(first)
        for n in range(1, 4):
            context = jnp.where(which == n, mix(first + n), context)
        context = context + matmul(new_w, nk_s[:, :latent])
        ctx_s[span, :] = context.astype(BF)

    def meta_copy(d, slot):
        tile = meta_v.at[fs, slot]
        return remote(tile, tile, meta_send.at[d], meta_recv.at[slot], lax.rem(me + d, peers))

    for i, route in enumerate(ROUTES):
        for n in range(2):
            cache_copy(i, n).wait()
        each(route.first // 16, (route.first + route.count) // 16, attend)
        if i == 0:
            out_copy.wait()
            gain = jnp.zeros((1, depth), F32)
            pad = jnp.zeros((wo_v.shape[0], WIDE - depth), BF)
            res_pad = jnp.zeros((16, WIDE - depth), F32)
            for j in range(peers):
                part = slice(j * depth, (j + 1) * depth)
                wo_s[j] = jnp.concatenate([wo_v[:, part], pad], axis=1)
                res = jnp.concatenate([res_ref[0, :, part].astype(F32)] * 4, axis=0)
                res_s[j] = jnp.concatenate([res, res_pad], axis=1)
                gain = jnp.where(me == j, gain_ref[:, part], gain)
            gain = jnp.concatenate([gain, jnp.zeros((1, WIDE - depth), F32)], axis=1)
            lane = lax.broadcasted_iota(jnp.int32, (1, rows), 1)
            here = lane // (STEPS * TOP) == lax.rem(me, 4)
            own_ids = jnp.where(here, spread(ids_ref[0].astype(F32), rows), 0.0)
            own_gates = jnp.where(here, spread(gates_ref[0], rows), 0.0)
            meta_v[fs, me] = jnp.concatenate(
                [own_ids, own_gates, jnp.zeros((6, rows), F32)], axis=0
            )
            pl.semaphore_wait(barrier, peers - 1 + groups - 1)
        values = matmul(ctx_s[route.rows, :], wv_ref[...]).astype(BF)
        owner = (route.first + lax.broadcasted_iota(jnp.int32, (route.count, 1), 0)) // STEPS
        own_token = owner == me
        together = 4 // route.line

        def project(n, route=route, values=values, own_token=own_token, head=heads[i]):
            spots = [(d, n * together + k) for k in range(together) for d in range(route.line)]
            for d, g in spots:
                j = place.plus(route.offset(d, g))
                part = matmul(values, wo_s[j])
                res = jnp.concatenate([res_s[j]] * (route.count // 16), axis=0)
                send_v[j, route.rows, :] = (part + jnp.where(own_token, res, 0.0)).astype(BF)
            for d, g in spots:
                if d > 0:
                    head.first(d, g).start()

        each(0, route.plane // together, project)
        if i == 0:
            each(1, peers, lambda d: meta_copy(d, me).start())

            def load(e):
                for n in range(3):
                    weight_copy(n, e).start()

            each(0, experts, load)

    each(1, peers, lambda d: meta_copy(d, lax.rem(me + d, peers)).wait_recv())
    for d in range(1, groups):
        group_copy(0, d, meta_v.at[fs]).start()

    for h in heads:
        each(1, h.route.plane, lambda g, h=h: h.step(g, att))
        h.step(0, att)
    for h in heads:
        each(1, h.route.plane, lambda g, h=h: h.add(g, att))

    attended = att[...]
    x_v[fs] = (attended * gain).astype(BF)
    for d in range(1, groups):
        group_copy(1, d, x_v.at[fs]).start()
    column = jnp.sum(attended * attended, -1, keepdims=True)
    row = jnp.sum(jnp.where(diagonal, column, 0.0), 0, keepdims=True)
    ssq_s[...] = jnp.broadcast_to(row, ssq_s.shape)

    def ssq_copy(d, slot):
        return remote(
            ssq_s, ssq_r.at[slot], ssq_send.at[d], ssq_recv.at[slot], lax.rem(me + d, peers)
        )

    each(1, peers, lambda d: ssq_copy(d, me).start())

    pair_lane = lax.broadcasted_iota(jnp.int32, (1, rows), 1)
    slot_c = lax.broadcasted_iota(jnp.int32, (rows, experts * block), 1)
    slot_r = lax.broadcasted_iota(jnp.int32, (experts * block, rows), 0)

    for q in range(groups):
        piece = lax.rem(fs + groups - q, groups)
        if q > 0:
            group_copy(0, q, meta_v.at[piece]).wait_recv()
            group_copy(1, q, x_v.at[piece]).wait_recv()

        def read_meta(n, piece=piece):
            info = meta_v[piece, 4 * n]
            for i in range(1, 4):
                info = info + meta_v[piece, 4 * n + i]
            j = piece * per + n
            code_s[j] = info[0:1, :].astype(jnp.int32) * block + pair_lane // TOP
            gate_s[j] = info[1:2, :]

        each(0, per, read_meta)
        x = x_v[piece][:, :depth]
        owners = pl.ds(pl.multiple_of(piece * per, per), per)

        def multiply(n, x=x, owners=owners, q=q):
            for e in (2 * n, 2 * n + 1):
                if q == 0:
                    weight_copy(0, e).wait()
                    weight_copy(1, e).wait()
                spot = pl.ds(pl.multiple_of(e * block, block), block)
                gate = matmul(x, wg_v[e]).astype(BF)
                up = matmul(x, wu_v[e]).astype(BF)
                dense[owners, spot, :half] = gate.reshape(per, block, half)
                dense[owners, spot, half:] = up.reshape(per, block, half)

        each(0, experts // 2, multiply)

        def pick(n, piece=piece):
            j = piece * per + lax.rem(n // NY, 2) * NY + lax.rem(place.y + n, NY)
            code = jnp.sum(jnp.where(diagonal, code_s[j], 0), 1, keepdims=True)
            chosen = (code == slot_c).astype(F32).astype(BF)
            part_v[j] = matmul(chosen, dense[j]).astype(BF)
            offset = (
                lax.rem(j // (NZ * NY) + NX - place.x, NX),
                lax.rem(lax.rem(j // NY, NZ) + NZ - place.z, NZ),
                lax.rem(lax.rem(j, NY) + NY - place.y, NY),
            )
            for s in sums:
                s.send(offset)

        each(0, per, pick)
        if q == 0:
            def add_ssq(d, total):
                slot = lax.rem(me + d, peers)
                ssq_copy(d, slot).wait_recv()
                return total + ssq_r[slot]

            sum_v[fs] = lax.fori_loop(1, peers, add_ssq, ssq_s[...])
            for d in range(1, groups):
                group_copy(2, d, sum_v.at[fs]).start()

    def turn(p):
        return lax.rem(fs + groups - p, groups)

    z_half = place.z // 2
    x_first = jnp.where(turn(z_half) < turn(2 + z_half), 0, 1)
    h_first = jnp.where(turn(2 * place.x) < turn(2 * place.x + 1), 0, 1)

    def z_order(i):
        x = lax.rem(x_first + i // NY, NX)
        return lax.rem(x + NX - place.x, NX) * NY + lax.rem(i, NY)

    def y_order(i):
        p = lax.rem(fs + groups - i // 2, groups)
        z = 2 * lax.rem(p, 2) + lax.rem(i, 2)
        return lax.rem(p // 2 + NX - place.x, NX) * NZ + lax.rem(z + NZ - place.z, NZ)

    def x_order(i):
        z = 2 * lax.rem(h_first + i // 8, 2) + lax.rem(i // NY, 2)
        return lax.rem(z + NZ - place.z, NZ) * NY + lax.rem(i, NY)

    def relay(i):
        sums[0].step(z_order(i), acc)
        sums[1].step(y_order(i), acc)
        sums[2].step(x_order(2 * i), acc)
        sums[2].step(x_order(2 * i + 1), acc)

    each(0, ROUTES[0].plane, relay)
    for s in sums:
        each(1, s.route.plane, lambda g, s=s: s.add(g, acc))

    for d in range(1, groups):
        group_copy(2, d, sum_v.at[from_group(d)]).wait_recv()
    token = block * lax.rem(me, per) + token_r // TOP
    squares = jnp.sum(jnp.where(token == token_c, sum_v[me // per][:1, :], 0.0), 1, keepdims=True)
    scale = lax.rsqrt(squares / (depth * peers) + 1e-06)
    weight = jnp.sum(jnp.where(diagonal, gate_s[me], 0.0), 1, keepdims=True)
    gate = acc[:, :half] * scale
    up = acc[:, half:] * scale
    hid_v[me] = (gate / (1.0 + jnp.exp(-gate)) * up * weight).astype(BF)

    for g in gathers:
        g.begin()
    for g in gathers:
        each(1, g.route.plane, g.relay)

    def expand(o):
        offset = offset_of(o)
        j = place.minus(offset)
        for g in gathers:
            g.arrive(offset)
        chosen = (code_s[j] == slot_r).astype(F32).astype(BF)
        full = matmul(chosen, hid_v[j]).astype(BF)
        spot = pl.ds(pl.multiple_of(j * block, block), block)
        dense[:, spot, :half] = full.reshape(experts, block, half)

    each(0, peers, expand)
    each(0, experts, lambda e: weight_copy(2, e).wait())

    def shares(piece):
        spot = pl.ds(pl.multiple_of(piece * tokens, tokens), tokens)

        def some(n, total):
            for k in range(8):
                e = 8 * n + k
                total = total + lax.dot_general(
                    dense[e, spot, :half], wd_v[e], NT, preferred_element_type=F32
                )
            return total

        return lax.fori_loop(0, experts // 8, some, jnp.zeros((tokens, depth), F32))

    def routed_copy(d):
        peer = lax.rem(fs + d, groups)
        return pltpu.make_async_remote_copy(
            src_ref=routed_v.at[peer],
            dst_ref=routed_r.at[d],
            send_sem=g_send.at[3, d],
            recv_sem=g_recv.at[3, d],
            device_id={"fsdp": peer},
            device_id_type=MESH,
        )

    for d in range(1, groups):
        peer = lax.rem(fs + d, groups)
        routed_v[peer, :, :depth] = shares(peer).astype(BF)
        routed_copy(d).start()
    mixed = att[:, :depth] + shares(fs)
    for d in range(1, groups):
        routed_copy(d).wait_recv()
        mixed = mixed + routed_r[d][:, :depth].astype(F32)
    for j in range(peers):
        home_s[j, :, :depth] = mixed[j * own_rows : (j + 1) * own_rows, :]

    def home_copy(d, slot):
        peer = lax.rem(me + d, peers)
        return remote(home_s.at[peer], home_r.at[slot], o_send.at[d], o_recv.at[slot], peer)

    each(1, peers, lambda d: home_copy(d, me).start())
    home_r[me] = home_s[me]
    for s in heads + sums + gathers:
        s.finish()
    for d in range(1, groups):
        routed_copy(d).wait_send()
        group_copy(0, d, meta_v.at[fs]).wait_send()
        group_copy(1, d, x_v.at[fs]).wait_send()
        group_copy(2, d, sum_v.at[fs]).wait_send()

    def close(d):
        ssq_copy(d, me).wait_send()
        meta_copy(d, me).wait_send()

    each(1, peers, close)
    each(1, peers, lambda d: home_copy(d, lax.rem(me + d, peers)).wait_recv())
    for j in range(peers):
        out_ref[0, :, j * depth : (j + 1) * depth] = home_r[j][:, :depth]
    each(1, peers, lambda d: home_copy(d, me).wait_send())


def shards(
    residual,
    gain,
    queries,
    new_keys,
    cache,
    lengths,
    w_value,
    w_out,
    w_gate,
    w_up,
    w_down,
    expert_ids,
    gates,
):
    peers = lax.axis_size("exp")
    groups = lax.axis_size("fsdp")
    group_rows, steps, _, key = queries.shape
    tokens = group_rows * steps
    experts, depth, half = w_gate.shape
    block = tokens * groups // peers
    rows = block * TOP
    smem, dma = pl.BlockSpec(memory_space=pltpu.SMEM), pltpu.SemaphoreType.DMA
    scratch = [
        pltpu.VMEM((peers, experts * block, 2 * half), BF),
        pltpu.VMEM(w_out.shape[1:], BF),
        pltpu.VMEM((peers, w_out.shape[1], WIDE), BF),
        pltpu.VMEM((peers, 16, WIDE), F32),
        pltpu.VMEM((tokens, key), BF),
        pltpu.VMEM((tokens, key), BF),
        pltpu.VMEM((tokens, tokens), F32),
        pltpu.VMEM((tokens, w_value.shape[1]), BF),
        pltpu.VMEM((peers, tokens, WIDE), BF),
        pltpu.VMEM((tokens, WIDE), F32),
        pltpu.VMEM((8, tokens), F32),
        pltpu.VMEM((peers, 8, tokens), F32),
        pltpu.VMEM((groups, 8, tokens), F32),
        pltpu.VMEM((groups, tokens, WIDE), BF),
        pltpu.VMEM((groups, peers, 8, rows), F32),
        pltpu.VMEM(w_gate.shape, BF),
        pltpu.VMEM(w_gate.shape, BF),
        pltpu.VMEM(w_gate.shape, BF),
        pltpu.VMEM((peers, rows, 2 * half), BF),
        pltpu.VMEM((rows, 2 * half), F32),
        pltpu.VMEM((peers, rows, half), BF),
        pltpu.VMEM((peers, 1, rows), jnp.int32),
        pltpu.VMEM((peers, 1, rows), F32),
        pltpu.VMEM((groups, tokens, WIDE), BF),
        pltpu.VMEM((groups, tokens, WIDE), BF),
        pltpu.VMEM((peers, steps, WIDE), F32),
        pltpu.VMEM((peers, steps, WIDE), F32),
        dma((len(ROUTES), 2)),
        dma,
        dma((3, experts)),
        dma((peers,)),
        dma((peers,)),
        dma((peers,)),
        dma((peers,)),
        dma((4, groups)),
        dma((4, groups)),
        dma((peers,)),
        dma((peers,)),
    ]
    for route in ROUTES:
        scratch += reduce_scratch(route, WIDE)
    for route in ROUTES:
        scratch += reduce_scratch(route, 2 * half)
    for route in ROUTES:
        scratch += gather_scratch(route)
    return pl.pallas_call(
        functools.partial(layer_kernel, peers, groups),
        out_shape=jax.ShapeDtypeStruct(residual.shape, F32),
        in_specs=[smem, vmem(), vmem(), anywhere(), vmem(), anywhere()]
        + [vmem()] * 4
        + [anywhere()] * 3,
        out_specs=vmem(),
        scratch_shapes=scratch,
        compiler_params=pltpu.CompilerParams(
            collective_id=0, has_side_effects=True, vmem_limit_bytes=HIGH
        ),
        name="layer",
    )(
        lengths,
        queries[:, :, 0, :],
        new_keys,
        cache,
        w_value[0],
        w_out[0],
        residual,
        gain.reshape(1, -1),
        expert_ids,
        gates,
        w_gate,
        w_up,
        w_down,
    )


def solution(mesh):
    return jax.shard_map(
        shards,
        mesh=mesh,
        in_specs=(
            P(("fsdp", "exp"), None, None),
            P(),
            P("fsdp", None, "exp", None),
            P("fsdp", None, None),
            P("fsdp", None, None),
            P("fsdp"),
            P("exp", None, None),
            P("exp", None, None),
            P(None, "exp", "fsdp"),
            P(None, "exp", "fsdp"),
            P(None, "exp", "fsdp"),
            P(("fsdp", "exp"), None, None),
            P(("fsdp", "exp"), None, None),
        ),
        out_specs=P(("fsdp", "exp"), None, None),
        check_vma=False,
    )
```

time: 167 us -> 133 us (0.80)
  Pallas kernels: 164 us -> 131 us
    pallas_call x2 -> x1, Pallas kernels: 164 us -> 131 us  [shards(): pl.pallas_call(functools.partial(layer_kernel, peers, groups), out_shape=...]
where the time goes in v3:
time: 133 us
  Pallas kernels  131 us (98%)
  local copies, waits for them, and re-layouts  1.55 us (1%)
    pallas_call x1, Pallas kernels, shards(): pl.pallas_call(functools.partial(layer_kernel, peers, groups), out_shape=...  131 us

profile of v3, /device:TPU:1, one launch (start us, length us, event | category | flops | bytes accessed | tf_op | source)
XLA Modules:
  0.0 132.6 jit_solution(16362309837159207340)
XLA Ops:
  0.0 131.0 %layer.1 = f32[1,4,7168]{2,1,0:T(4,128)} custom-call(s32[32]{0:T(128)} %refs_0_.1, bf16[32,4,576]{2,1,0:T(4,128)(2,1)} %bitcast.5, bf16[32,4,576]{2,1,0:T(4,128)(2,1)} %refs_2_.1, bf16[32,576,256]{2,1,0:T(8,128)(2,1)} %refs_3_.1, bf16[512,128]{1,0:T(8,128)(2,1)} %bitcast.6, bf16[128,7168]{1,0:T(8,128)(2,1)} %bitcast.4, bf16[1,4,7168]{2,1,0:T(4,128)(2,1)} %refs_6_.1, ...), custom_call_target="tpu_custom_call" | custom-call | tf_op jit(solution)/shard_map/layer/pallas_call | solution.py:753
  131.0 1.6 %copy.15 = f32[1,4,7168]{2,1,0:T(4,128)} copy(f32[1,4,7168]{2,1,0:T(4,128)} %layer.1) | data formatting | bytes 229376

commit v4 on v3

--- a/solution.py
+++ b/solution.py
@@ -31,15 +31,6 @@
     return pl.BlockSpec(memory_space=pl.ANY)
 
 
-def greet(barrier, axis, me, size):
-    def one(d):
-        pl.semaphore_signal(
-            barrier, inc=1, device_id={axis: lax.rem(me + d, size)}, device_id_type=MESH
-        )
-
-    each(1, size, one)
-
-
 def each(lower, upper, body):
     def step(i, carry):
         body(i)
@@ -114,9 +105,9 @@
         route = self.route
         return remote(
             self.src.at[self.place.plus(route.offset(d, g)), route.rows],
-            self.got.at[d - 1, g],
-            self.s1.at[d - 1, g],
-            self.r1.at[d - 1, g],
+            self.got.at[g, d - 1],
+            self.s1,
+            self.r1.at[g],
             self.place.plus(route.offset(d, 0)),
         )
 
@@ -124,8 +115,8 @@
         return remote(
             self.out.at[g],
             self.fin.at[g],
-            self.s2.at[g],
-            self.r2.at[g],
+            self.s2,
+            self.r2,
             self.place.plus(self.route.offset(0, g)),
         )
 
@@ -136,51 +127,49 @@
         def _():
             self.first(d, g).start()
 
-    def combined(self, g):
+    def step(self, g, acc_ref):
         route = self.route
+        got = self.got.at[g]
+        remote(got, got, self.s1, self.r1.at[g], self.place.me).wait_recv()
         total = self.src[self.place.plus(route.offset(0, g)), route.rows].astype(F32)
         for d in range(1, route.line):
-            self.first(d, g).wait_recv()
-            total = total + self.got[d - 1, g].astype(F32)
-        return total
-
-    def add(self, g, acc_ref):
-        self.second(g).wait_recv()
-        acc_ref[self.route.rows] += self.fin[g].astype(F32)
-
-    def step(self, g, acc_ref):
-        total = self.combined(g)
+            total = total + self.got[g, d - 1].astype(F32)
 
         @pl.when(g == 0)
         def _():
-            acc_ref[self.route.rows] = total
+            acc_ref[route.rows] = total
 
         @pl.when(g != 0)
         def _():
             self.out[g] = total.astype(BF)
             self.second(g).start()
 
+    def add(self, acc_ref):
+        route = self.route
+        rest = self.fin.at[pl.ds(1, route.plane - 1)]
+        remote(rest, rest, self.s2, self.r2, self.place.me).wait_recv()
+        total = acc_ref[route.rows]
+        for g in range(1, route.plane):
+            total = total + self.fin[g].astype(F32)
+        acc_ref[route.rows] = total
+
     def finish(self):
-        route = self.route
-
-        def one(g):
-            for d in range(1, route.line):
-                self.first(d, g).wait_send()
-
-        each(0, route.plane, one)
-        each(1, route.plane, lambda g: self.second(g).wait_send())
+        rest = self.out.at[pl.ds(1, self.route.plane - 1)]
+        remote(self.got, self.got, self.s1, self.r1.at[0], self.place.me).wait_send()
+        remote(rest, rest, self.s2, self.r2, self.place.me).wait_send()
 
 
 def reduce_scratch(route, cols):
     lines, plane = route.line - 1, route.plane
+    dma = pltpu.SemaphoreType.DMA
     return [
-        pltpu.VMEM((lines, plane, route.count, cols), BF),
+        pltpu.VMEM((plane, lines, route.count, cols), BF),
         pltpu.VMEM((plane, route.count, cols), BF),
         pltpu.VMEM((plane, route.count, cols), BF),
-        pltpu.SemaphoreType.DMA((lines, plane)),
-        pltpu.SemaphoreType.DMA((lines, plane)),
-        pltpu.SemaphoreType.DMA((plane,)),
-        pltpu.SemaphoreType.DMA((plane,)),
+        dma,
+        dma((plane,)),
+        dma,
+        dma,
     ]
 
 
@@ -192,17 +181,13 @@
     def near(self, g, source):
         block = self.whole.at[source, self.route.rows]
         return remote(
-            block, block, self.s1.at[g], self.r.at[0, g], self.place.plus(self.route.offset(0, g))
+            block, block, self.s1, self.r.at[0, g], self.place.plus(self.route.offset(0, g))
         )
 
     def far(self, d, g, source):
         block = self.whole.at[source, self.route.rows]
         return remote(
-            block,
-            block,
-            self.s2.at[d - 1, g],
-            self.r.at[d, g],
-            self.place.plus(self.route.offset(d, 0)),
+            block, block, self.s2, self.r.at[d, g], self.place.plus(self.route.offset(d, 0))
         )
 
     def begin(self):
@@ -227,23 +212,14 @@
 
     def finish(self):
         route = self.route
-
-        def one(g):
-            source = self.place.minus(route.offset(0, g))
-            for d in range(1, route.line):
-                self.far(d, g, source).wait_send()
-
-        each(0, route.plane, one)
-        each(1, route.plane, lambda g: self.near(g, self.place.me).wait_send())
+        for sem, count in ((self.s1, route.plane - 1), (self.s2, (route.line - 1) * route.plane)):
+            blocks = self.whole.at[pl.ds(0, count), route.rows]
+            remote(blocks, blocks, sem, self.r.at[0, 0], self.place.me).wait_send()
 
 
 def gather_scratch(route):
-    lines, plane = route.line - 1, route.plane
-    return [
-        pltpu.SemaphoreType.DMA((plane,)),
-        pltpu.SemaphoreType.DMA((lines, plane)),
-        pltpu.SemaphoreType.DMA((route.line, plane)),
-    ]
+    dma = pltpu.SemaphoreType.DMA
+    return [dma, dma, dma((route.line, route.plane))]
 
 
 def offset_of(o):
@@ -303,15 +279,12 @@
         cache_sem,
         wo_sem,
         w_sem,
-        ssq_send,
-        ssq_recv,
-        meta_send,
-        meta_recv,
+        ssq_sem,
+        meta_sem,
+        home_sem,
         g_send,
         g_recv,
-        o_send,
-        o_recv,
-    ) = refs[:52]
+    ) = refs[:49]
     place = Place()
     me = place.me
     fs = lax.axis_index("fsdp")
@@ -323,7 +296,18 @@
     per = peers // groups
     own_rows = home_s.shape[1]
     barrier = pltpu.get_barrier_semaphore()
-    rest = refs[52:]
+
+    def greet(axis, mine, size):
+        def one(d):
+            pl.semaphore_signal(
+                barrier, inc=1, device_id={axis: lax.rem(mine + d, size)}, device_id_type=MESH
+            )
+
+        each(1, size, one)
+
+    greet("exp", me, peers)
+    greet("fsdp", fs, groups)
+    rest = refs[49:]
     heads = [Reduce(place, r, send_v, rest[7 * i : 7 * i + 7]) for i, r in enumerate(ROUTES)]
     rest = rest[7 * len(ROUTES) :]
     sums = [Reduce(place, r, part_v, rest[7 * i : 7 * i + 7]) for i, r in enumerate(ROUTES)]
@@ -355,10 +339,10 @@
             dst = dense.at[span, pl.ds(0, left), pl.ds(positions, positions)]
         return pltpu.make_async_copy(src, dst, cache_sem.at[i, n])
 
-    def weight_copy(n, e):
+    def weight_copy(n):
         src = (wg_ref, wu_ref, wd_ref)[n]
         dst = (wg_v, wu_v, wd_v)[n]
-        return pltpu.make_async_copy(src.at[e], dst.at[e], w_sem.at[n, e])
+        return pltpu.make_async_copy(src, dst, w_sem.at[n])
 
     out_copy = pltpu.make_async_copy(wo_ref, wo_v, wo_sem)
     for n in range(2):
@@ -367,8 +351,6 @@
     for i in range(1, len(ROUTES)):
         for n in range(2):
             cache_copy(i, n).start()
-    greet(barrier, "exp", me, peers)
-    greet(barrier, "fsdp", fs, groups)
 
     for b in range(tokens // 16):
         span = slice(b * 16, b * 16 + 16)
@@ -425,9 +407,13 @@
         context = context + matmul(new_w, nk_s[:, :latent])
         ctx_s[span, :] = context.astype(BF)
 
-    def meta_copy(d, slot):
-        tile = meta_v.at[fs, slot]
-        return remote(tile, tile, meta_send.at[d], meta_recv.at[slot], lax.rem(me + d, peers))
+    def meta_copy(d):
+        tile = meta_v.at[fs, me]
+        return remote(tile, tile, meta_sem.at[0], meta_sem.at[1], lax.rem(me + d, peers))
+
+    def all_copies(buffer, sem):
+        tiles = buffer.at[pl.ds(0, peers - 1)]
+        return remote(tiles, tiles, sem.at[0], sem.at[1], me)
 
     for i, route in enumerate(ROUTES):
         for n in range(2):
@@ -471,15 +457,11 @@
 
         each(0, route.plane // together, project)
         if i == 0:
-            each(1, peers, lambda d: meta_copy(d, me).start())
-
-            def load(e):
-                for n in range(3):
-                    weight_copy(n, e).start()
-
-            each(0, experts, load)
-
-    each(1, peers, lambda d: meta_copy(d, lax.rem(me + d, peers)).wait_recv())
+            each(1, peers, lambda d: meta_copy(d).start())
+            for n in range(3):
+                weight_copy(n).start()
+
+    all_copies(meta_v.at[fs], meta_sem).wait_recv()
     for d in range(1, groups):
         group_copy(0, d, meta_v.at[fs]).start()
 
@@ -487,7 +469,7 @@
         each(1, h.route.plane, lambda g, h=h: h.step(g, att))
         h.step(0, att)
     for h in heads:
-        each(1, h.route.plane, lambda g, h=h: h.add(g, att))
+        h.add(att)
 
     attended = att[...]
     x_v[fs] = (attended * gain).astype(BF)
@@ -497,24 +479,20 @@
     row = jnp.sum(jnp.where(diagonal, column, 0.0), 0, keepdims=True)
     ssq_s[...] = jnp.broadcast_to(row, ssq_s.shape)
 
-    def ssq_copy(d, slot):
-        return remote(
-            ssq_s, ssq_r.at[slot], ssq_send.at[d], ssq_recv.at[slot], lax.rem(me + d, peers)
-        )
-
-    each(1, peers, lambda d: ssq_copy(d, me).start())
+    def ssq_copy(d):
+        return remote(ssq_s, ssq_r.at[d], ssq_sem.at[0], ssq_sem.at[1], lax.rem(me + d, peers))
+
+    ssq_r[0] = ssq_s[...]
+    each(1, peers, lambda d: ssq_copy(d).start())
 
     pair_lane = lax.broadcasted_iota(jnp.int32, (1, rows), 1)
     slot_c = lax.broadcasted_iota(jnp.int32, (rows, experts * block), 1)
     slot_r = lax.broadcasted_iota(jnp.int32, (experts * block, rows), 0)
 
-    for q in range(groups):
-        piece = lax.rem(fs + groups - q, groups)
-        if q > 0:
-            group_copy(0, q, meta_v.at[piece]).wait_recv()
-            group_copy(1, q, x_v.at[piece]).wait_recv()
-
-        def read_meta(n, piece=piece):
+    def read_meta(q):
+        piece = from_group(q)
+
+        def one(n):
             info = meta_v[piece, 4 * n]
             for i in range(1, 4):
                 info = info + meta_v[piece, 4 * n + i]
@@ -522,76 +500,78 @@
             code_s[j] = info[0:1, :].astype(jnp.int32) * block + pair_lane // TOP
             gate_s[j] = info[1:2, :]
 
-        each(0, per, read_meta)
-        x = x_v[piece][:, :depth]
-        owners = pl.ds(pl.multiple_of(piece * per, per), per)
-
-        def multiply(n, x=x, owners=owners, q=q):
+        each(0, per, one)
+
+    def multiply(first, count, x):
+        def some(n):
             for e in (2 * n, 2 * n + 1):
-                if q == 0:
-                    weight_copy(0, e).wait()
-                    weight_copy(1, e).wait()
                 spot = pl.ds(pl.multiple_of(e * block, block), block)
                 gate = matmul(x, wg_v[e]).astype(BF)
                 up = matmul(x, wu_v[e]).astype(BF)
-                dense[owners, spot, :half] = gate.reshape(per, block, half)
-                dense[owners, spot, half:] = up.reshape(per, block, half)
-
-        each(0, experts // 2, multiply)
-
-        def pick(n, piece=piece):
-            j = piece * per + lax.rem(n // NY, 2) * NY + lax.rem(place.y + n, NY)
-            code = jnp.sum(jnp.where(diagonal, code_s[j], 0), 1, keepdims=True)
-            chosen = (code == slot_c).astype(F32).astype(BF)
-            part_v[j] = matmul(chosen, dense[j]).astype(BF)
-            offset = (
-                lax.rem(j // (NZ * NY) + NX - place.x, NX),
-                lax.rem(lax.rem(j // NY, NZ) + NZ - place.z, NZ),
-                lax.rem(lax.rem(j, NY) + NY - place.y, NY),
-            )
-            for s in sums:
-                s.send(offset)
-
-        each(0, per, pick)
-        if q == 0:
-            def add_ssq(d, total):
-                slot = lax.rem(me + d, peers)
-                ssq_copy(d, slot).wait_recv()
-                return total + ssq_r[slot]
-
-            sum_v[fs] = lax.fori_loop(1, peers, add_ssq, ssq_s[...])
-            for d in range(1, groups):
-                group_copy(2, d, sum_v.at[fs]).start()
-
-    def turn(p):
-        return lax.rem(fs + groups - p, groups)
-
-    z_half = place.z // 2
-    x_first = jnp.where(turn(z_half) < turn(2 + z_half), 0, 1)
-    h_first = jnp.where(turn(2 * place.x) < turn(2 * place.x + 1), 0, 1)
-
-    def z_order(i):
-        x = lax.rem(x_first + i // NY, NX)
-        return lax.rem(x + NX - place.x, NX) * NY + lax.rem(i, NY)
-
-    def y_order(i):
-        p = lax.rem(fs + groups - i // 2, groups)
-        z = 2 * lax.rem(p, 2) + lax.rem(i, 2)
-        return lax.rem(p // 2 + NX - place.x, NX) * NZ + lax.rem(z + NZ - place.z, NZ)
-
-    def x_order(i):
-        z = 2 * lax.rem(h_first + i // 8, 2) + lax.rem(i // NY, 2)
-        return lax.rem(z + NZ - place.z, NZ) * NY + lax.rem(i, NY)
-
-    def relay(i):
-        sums[0].step(z_order(i), acc)
-        sums[1].step(y_order(i), acc)
-        sums[2].step(x_order(2 * i), acc)
-        sums[2].step(x_order(2 * i + 1), acc)
-
-    each(0, ROUTES[0].plane, relay)
+                dense[first : first + count, spot, :half] = gate.reshape(count, block, half)
+                dense[first : first + count, spot, half:] = up.reshape(count, block, half)
+
+        each(0, experts // 2, some)
+
+    def pick(i):
+        q = i // per
+        n = lax.rem(i // NY, 2) * NY + lax.rem(place.y + i, NY)
+        j = from_group(q) * per + n
+        code = jnp.sum(jnp.where(diagonal, code_s[j], 0), 1, keepdims=True)
+        chosen = (code == slot_c).astype(F32).astype(BF)
+        part_v[j] = matmul(chosen, dense[q * per + n]).astype(BF)
+        offset = (
+            lax.rem(j // (NZ * NY) + NX - place.x, NX),
+            lax.rem(lax.rem(j // NY, NZ) + NZ - place.z, NZ),
+            lax.rem(lax.rem(j, NY) + NY - place.y, NY),
+        )
+        for s in sums:
+            s.send(offset)
+
+    def relay(q):
+        p = from_group(q)
+        x_off = lax.rem(p // 2 + NX - place.x, NX)
+        z_low = 2 * lax.rem(p, 2)
+
+        def z_off(i):
+            return lax.rem(z_low + i + NZ - place.z, NZ)
+
+        @pl.when(lax.rem(p, 2) == place.z // 2)
+        def _():
+            each(0, NY, lambda i: sums[0].step(x_off * NY + i, acc))
+
+        each(0, 2, lambda i: sums[1].step(x_off * NZ + z_off(i), acc))
+
+        @pl.when(x_off == 0)
+        def _():
+            each(0, 2 * NY, lambda i: sums[2].step(z_off(i // NY) * NY + lax.rem(i, NY), acc))
+
+    read_meta(0)
+    weight_copy(0).wait()
+    weight_copy(1).wait()
+    multiply(0, per, x_v[fs][:, :depth])
+    each(0, per, pick)
+
+    all_copies(ssq_r.at[pl.ds(1, peers - 1)], ssq_sem).wait_recv()
+    sum_v[fs] = jnp.sum(ssq_r[...], axis=0)
+    for d in range(1, groups):
+        group_copy(2, d, sum_v.at[fs]).start()
+    for q in range(1, groups):
+        group_copy(0, q, meta_v.at[from_group(q)]).wait_recv()
+        group_copy(1, q, x_v.at[from_group(q)]).wait_recv()
+        read_meta(q)
+    others = [x_v[from_group(q)][:, :depth] for q in range(1, groups)]
+    multiply(per, peers - per, jnp.concatenate(others, axis=0))
+    each(per, 2 * per, pick)
+    relay(0)
+    each(2 * per, 3 * per, pick)
+    relay(1)
+    each(3 * per, peers, pick)
+    relay(2)
+    relay(3)
+
     for s in sums:
-        each(1, s.route.plane, lambda g, s=s: s.add(g, acc))
+        s.add(acc)
 
     for d in range(1, groups):
         group_copy(2, d, sum_v.at[from_group(d)]).wait_recv()
@@ -619,20 +599,20 @@
         dense[:, spot, :half] = full.reshape(experts, block, half)
 
     each(0, peers, expand)
-    each(0, experts, lambda e: weight_copy(2, e).wait())
-
-    def shares(piece):
-        spot = pl.ds(pl.multiple_of(piece * tokens, tokens), tokens)
+    weight_copy(2).wait()
+
+    def shares(pieces):
+        spots = [pl.ds(pl.multiple_of(p * tokens, tokens), tokens) for p in pieces]
 
         def some(n, total):
-            for k in range(8):
-                e = 8 * n + k
-                total = total + lax.dot_general(
-                    dense[e, spot, :half], wd_v[e], NT, preferred_element_type=F32
-                )
+            for k in range(4):
+                e = 4 * n + k
+                both = jnp.concatenate([dense[e, spot, :half] for spot in spots], axis=0)
+                total = total + lax.dot_general(both, wd_v[e], NT, preferred_element_type=F32)
             return total
 
-        return lax.fori_loop(0, experts // 8, some, jnp.zeros((tokens, depth), F32))
+        start = jnp.zeros((len(pieces) * tokens, depth), F32)
+        return lax.fori_loop(0, experts // 4, some, start)
 
     def routed_copy(d):
         peer = lax.rem(fs + d, groups)
@@ -645,22 +625,27 @@
             device_id_type=MESH,
         )
 
-    for d in range(1, groups):
-        peer = lax.rem(fs + d, groups)
-        routed_v[peer, :, :depth] = shares(peer).astype(BF)
-        routed_copy(d).start()
-    mixed = att[:, :depth] + shares(fs)
+    mixed = att[:, :depth]
+    for pair in ((2, 3), (1, 0)):
+        both = shares([lax.rem(fs + d, groups) for d in pair])
+        for k, d in enumerate(pair):
+            share = both[k * tokens : (k + 1) * tokens]
+            if d > 0:
+                routed_v[lax.rem(fs + d, groups), :, :depth] = share.astype(BF)
+                routed_copy(d).start()
+            else:
+                mixed = mixed + share
     for d in range(1, groups):
         routed_copy(d).wait_recv()
         mixed = mixed + routed_r[d][:, :depth].astype(F32)
     for j in range(peers):
         home_s[j, :, :depth] = mixed[j * own_rows : (j + 1) * own_rows, :]
 
-    def home_copy(d, slot):
+    def home_copy(d):
         peer = lax.rem(me + d, peers)
-        return remote(home_s.at[peer], home_r.at[slot], o_send.at[d], o_recv.at[slot], peer)
-
-    each(1, peers, lambda d: home_copy(d, me).start())
+        return remote(home_s.at[peer], home_r.at[me], home_sem.at[0], home_sem.at[1], peer)
+
+    each(1, peers, lambda d: home_copy(d).start())
     home_r[me] = home_s[me]
     for s in heads + sums + gathers:
         s.finish()
@@ -670,15 +655,12 @@
         group_copy(1, d, x_v.at[fs]).wait_send()
         group_copy(2, d, sum_v.at[fs]).wait_send()
 
-    def close(d):
-        ssq_copy(d, me).wait_send()
-        meta_copy(d, me).wait_send()
-
-    each(1, peers, close)
-    each(1, peers, lambda d: home_copy(d, lax.rem(me + d, peers)).wait_recv())
+    all_copies(ssq_r, ssq_sem).wait_send()
+    all_copies(meta_v.at[fs], meta_sem).wait_send()
+    all_copies(home_s, home_sem).wait_recv()
     for j in range(peers):
         out_ref[0, :, j * depth : (j + 1) * depth] = home_r[j][:, :depth]
-    each(1, peers, lambda d: home_copy(d, me).wait_send())
+    all_copies(home_s, home_sem).wait_send()
 
 
 def shards(
@@ -734,15 +716,12 @@
         pltpu.VMEM((peers, steps, WIDE), F32),
         dma((len(ROUTES), 2)),
         dma,
-        dma((3, experts)),
-        dma((peers,)),
-        dma((peers,)),
-        dma((peers,)),
-        dma((peers,)),
+        dma((3,)),
+        dma((2,)),
+        dma((2,)),
+        dma((2,)),
         dma((4, groups)),
         dma((4, groups)),
-        dma((peers,)),
-        dma((peers,)),
     ]
     for route in ROUTES:
         scratch += reduce_scratch(route, WIDE)

time: 133 us -> 125 us (0.940)
  Pallas kernels: 131 us -> 124 us
    pallas_call x1, Pallas kernels: 131 us -> 124 us  [shards(): pl.pallas_call(functools.partial(layer_kernel, peers, groups), out_shape=...]
where the time goes in v4:
time: 125 us
  Pallas kernels  124 us (99%)
  local copies, waits for them, and re-layouts  1.55 us (1%)
    pallas_call x1, Pallas kernels, shards(): pl.pallas_call(functools.partial(layer_kernel, peers, groups), out_shape=...  124 us

profile of v4, /device:TPU:1, one launch (start us, length us, event | category | flops | bytes accessed | tf_op | source)
XLA Modules:
  0.0 125.1 jit_solution(5743799445177870445)
XLA Ops:
  0.0 123.6 %layer.1 = f32[1,4,7168]{2,1,0:T(4,128)} custom-call(s32[32]{0:T(128)} %refs_0_.1, bf16[32,4,576]{2,1,0:T(4,128)(2,1)} %bitcast.5, bf16[32,4,576]{2,1,0:T(4,128)(2,1)} %refs_2_.1, bf16[32,576,256]{2,1,0:T(8,128)(2,1)} %refs_3_.1, bf16[512,128]{1,0:T(8,128)(2,1)} %bitcast.6, bf16[128,7168]{1,0:T(8,128)(2,1)} %bitcast.4, bf16[1,4,7168]{2,1,0:T(4,128)(2,1)} %refs_6_.1, ...), custom_call_target="tpu_custom_call" | custom-call | tf_op jit(solution)/shard_map/layer/pallas_call | solution.py:732
  123.6 1.6 %copy.15 = f32[1,4,7168]{2,1,0:T(4,128)} copy(f32[1,4,7168]{2,1,0:T(4,128)} %layer.1) | data formatting | bytes 229376

commit v5 on v4

--- a/solution.py
+++ b/solution.py
@@ -14,7 +14,7 @@
 BF = jnp.bfloat16
 F32 = jnp.float32
 WIDE = 256
-HIGH = 58 * 1024 * 1024
+HIGH = 60 * 1024 * 1024
 NX, NZ, NY = 2, 4, 4
 NT = (((1,), (1,)), ((), ()))
 
@@ -270,7 +270,7 @@
         part_v,
         acc,
         hid_v,
-        code_s,
+        spread_s,
         gate_s,
         routed_v,
         routed_r,
@@ -419,6 +419,10 @@
         for n in range(2):
             cache_copy(i, n).wait()
         each(route.first // 16, (route.first + route.count) // 16, attend)
+    for n in range(3):
+        weight_copy(n).start()
+
+    for i, route in enumerate(ROUTES):
         if i == 0:
             out_copy.wait()
             gain = jnp.zeros((1, depth), F32)
@@ -458,8 +462,6 @@
         each(0, route.plane // together, project)
         if i == 0:
             each(1, peers, lambda d: meta_copy(d).start())
-            for n in range(3):
-                weight_copy(n).start()
 
     all_copies(meta_v.at[fs], meta_sem).wait_recv()
     for d in range(1, groups):
@@ -468,6 +470,30 @@
     for h in heads:
         each(1, h.route.plane, lambda g, h=h: h.step(g, att))
         h.step(0, att)
+    pair_lane = lax.broadcasted_iota(jnp.int32, (1, rows), 1)
+    slot_c = lax.broadcasted_iota(jnp.int32, (rows, experts * block), 1)
+    slot_r = lax.broadcasted_iota(jnp.int32, (experts * block, rows), 0)
+
+    def read_meta(q):
+        piece = from_group(q)
+
+        def one(n):
+            info = meta_v[piece, 4 * n]
+            for i in range(1, 4):
+                info = info + meta_v[piece, 4 * n + i]
+            j = piece * per + n
+            code = info[0:1, :].astype(jnp.int32) * block + pair_lane // TOP
+            spread_s[j] = (code == slot_r).astype(F32).astype(BF)
+            code = jnp.sum(jnp.where(diagonal, code, 0), 1, keepdims=True)
+            part_v[j] = (code == slot_c).astype(F32).astype(BF)
+            gate_s[j] = info[1:2, :]
+
+        each(0, per, one)
+
+    read_meta(0)
+    for q in range(1, groups):
+        group_copy(0, q, meta_v.at[from_group(q)]).wait_recv()
+        read_meta(q)
     for h in heads:
         h.add(att)
 
@@ -485,48 +511,37 @@
     ssq_r[0] = ssq_s[...]
     each(1, peers, lambda d: ssq_copy(d).start())
 
-    pair_lane = lax.broadcasted_iota(jnp.int32, (1, rows), 1)
-    slot_c = lax.broadcasted_iota(jnp.int32, (rows, experts * block), 1)
-    slot_r = lax.broadcasted_iota(jnp.int32, (experts * block, rows), 0)
-
-    def read_meta(q):
-        piece = from_group(q)
-
-        def one(n):
-            info = meta_v[piece, 4 * n]
-            for i in range(1, 4):
-                info = info + meta_v[piece, 4 * n + i]
-            j = piece * per + n
-            code_s[j] = info[0:1, :].astype(jnp.int32) * block + pair_lane // TOP
-            gate_s[j] = info[1:2, :]
-
-        each(0, per, one)
-
     def multiply(first, count, x):
         def some(n):
-            for e in (2 * n, 2 * n + 1):
+            for e in [4 * n + k for k in range(4)]:
                 spot = pl.ds(pl.multiple_of(e * block, block), block)
                 gate = matmul(x, wg_v[e]).astype(BF)
                 up = matmul(x, wu_v[e]).astype(BF)
                 dense[first : first + count, spot, :half] = gate.reshape(count, block, half)
                 dense[first : first + count, spot, half:] = up.reshape(count, block, half)
 
-        each(0, experts // 2, some)
+        each(0, experts // 4, some)
 
     def pick(i):
-        q = i // per
-        n = lax.rem(i // NY, 2) * NY + lax.rem(place.y + i, NY)
-        j = from_group(q) * per + n
-        code = jnp.sum(jnp.where(diagonal, code_s[j], 0), 1, keepdims=True)
-        chosen = (code == slot_c).astype(F32).astype(BF)
-        part_v[j] = matmul(chosen, dense[q * per + n]).astype(BF)
-        offset = (
-            lax.rem(j // (NZ * NY) + NX - place.x, NX),
-            lax.rem(lax.rem(j // NY, NZ) + NZ - place.z, NZ),
-            lax.rem(lax.rem(j, NY) + NY - place.y, NY),
-        )
-        for s in sums:
-            s.send(offset)
+        found = []
+        for k in range(2):
+            q = (2 * i + k) // per
+            n = lax.rem((2 * i + k) // NY, 2) * NY + lax.rem(place.y + 2 * i + k, NY)
+            j = from_group(q) * per + n
+            found.append((j, matmul(part_v[j], dense[q * per + n]).astype(BF)))
+        for j, part in found:
+            part_v[j] = part
+        for j, _ in found:
+            offset = (
+                lax.rem(j // (NZ * NY) + NX - place.x, NX),
+                lax.rem(lax.rem(j // NY, NZ) + NZ - place.z, NZ),
+                lax.rem(lax.rem(j, NY) + NY - place.y, NY),
+            )
+            for s in sums:
+                s.send(offset)
+
+    def pick_group(q):
+        each(q * per // 2, (q + 1) * per // 2, pick)
 
     def relay(q):
         p = from_group(q)
@@ -546,27 +561,24 @@
         def _():
             each(0, 2 * NY, lambda i: sums[2].step(z_off(i // NY) * NY + lax.rem(i, NY), acc))
 
-    read_meta(0)
     weight_copy(0).wait()
     weight_copy(1).wait()
     multiply(0, per, x_v[fs][:, :depth])
-    each(0, per, pick)
+    pick_group(0)
 
     all_copies(ssq_r.at[pl.ds(1, peers - 1)], ssq_sem).wait_recv()
     sum_v[fs] = jnp.sum(ssq_r[...], axis=0)
     for d in range(1, groups):
         group_copy(2, d, sum_v.at[fs]).start()
     for q in range(1, groups):
-        group_copy(0, q, meta_v.at[from_group(q)]).wait_recv()
         group_copy(1, q, x_v.at[from_group(q)]).wait_recv()
-        read_meta(q)
     others = [x_v[from_group(q)][:, :depth] for q in range(1, groups)]
     multiply(per, peers - per, jnp.concatenate(others, axis=0))
-    each(per, 2 * per, pick)
+    pick_group(1)
     relay(0)
-    each(2 * per, 3 * per, pick)
+    pick_group(2)
     relay(1)
-    each(3 * per, peers, pick)
+    pick_group(3)
     relay(2)
     relay(3)
 
@@ -588,17 +600,18 @@
     for g in gathers:
         each(1, g.route.plane, g.relay)
 
-    def expand(o):
-        offset = offset_of(o)
-        j = place.minus(offset)
-        for g in gathers:
-            g.arrive(offset)
-        chosen = (code_s[j] == slot_r).astype(F32).astype(BF)
-        full = matmul(chosen, hid_v[j]).astype(BF)
-        spot = pl.ds(pl.multiple_of(j * block, block), block)
-        dense[:, spot, :half] = full.reshape(experts, block, half)
-
-    each(0, peers, expand)
+    def expand(n):
+        offsets = [offset_of(2 * n), offset_of(2 * n + 1)]
+        for offset in offsets:
+            for g in gathers:
+                g.arrive(offset)
+        blocks = [place.minus(offset) for offset in offsets]
+        full = [matmul(spread_s[j], hid_v[j]).astype(BF) for j in blocks]
+        for j, rows_of in zip(blocks, full):
+            spot = pl.ds(pl.multiple_of(j * block, block), block)
+            dense[:, spot, :half] = rows_of.reshape(experts, block, half)
+
+    each(0, peers // 2, expand)
     weight_copy(2).wait()
 
     def shares(pieces):
@@ -708,7 +721,7 @@
         pltpu.VMEM((peers, rows, 2 * half), BF),
         pltpu.VMEM((rows, 2 * half), F32),
         pltpu.VMEM((peers, rows, half), BF),
-        pltpu.VMEM((peers, 1, rows), jnp.int32),
+        pltpu.VMEM((peers, experts * block, rows), BF),
         pltpu.VMEM((peers, 1, rows), F32),
         pltpu.VMEM((groups, tokens, WIDE), BF),
         pltpu.VMEM((groups, tokens, WIDE), BF),

time: 125 us -> 124 us (level)
  no operation moved by 1% of the time
where the time goes in v5:
time: 124 us
  Pallas kernels  123 us (99%)
  local copies, waits for them, and re-layouts  1.55 us (1%)
    pallas_call x1, Pallas kernels, shards(): pl.pallas_call(functools.partial(layer_kernel, peers, groups), out_shape=...  123 us

profile of v5, /device:TPU:1, one launch (start us, length us, event | category | flops | bytes accessed | tf_op | source)
XLA Modules:
  0.0 124.3 jit_solution(14243557194159279377)
XLA Ops:
  0.0 122.7 %layer.1 = f32[1,4,7168]{2,1,0:T(4,128)} custom-call(s32[32]{0:T(128)} %refs_0_.1, bf16[32,4,576]{2,1,0:T(4,128)(2,1)} %bitcast.5, bf16[32,4,576]{2,1,0:T(4,128)(2,1)} %refs_2_.1, bf16[32,576,256]{2,1,0:T(8,128)(2,1)} %refs_3_.1, bf16[512,128]{1,0:T(8,128)(2,1)} %bitcast.6, bf16[128,7168]{1,0:T(8,128)(2,1)} %bitcast.4, bf16[1,4,7168]{2,1,0:T(4,128)(2,1)} %refs_6_.1, ...), custom_call_target="tpu_custom_call" | custom-call | tf_op jit(solution)/shard_map/layer/pallas_call | solution.py:745
  122.7 1.6 %copy.15 = f32[1,4,7168]{2,1,0:T(4,128)} copy(f32[1,4,7168]{2,1,0:T(4,128)} %layer.1) | data formatting | bytes 229376

commit v6 on v5

--- a/solution.py
+++ b/solution.py
@@ -83,6 +83,7 @@
 
 
 ROUTES = (Route("z", 0, 48), Route("y", 48, 48), Route("x", 96, 32))
+HEAD_ROUTES = (Route("z", 0, 80), Route("y", 80, 80), Route("x", 160, 64))
 
 
 def remote(src, dst, send, recv, peer):
@@ -251,13 +252,15 @@
         out_ref,
         dense,
         wo_v,
-        wo_s,
+        wo_t,
         res_s,
+        res_r,
         q_s,
         nk_s,
         new_s,
         ctx_s,
         send_v,
+        att_t,
         att,
         ssq_s,
         ssq_r,
@@ -281,10 +284,11 @@
         w_sem,
         ssq_sem,
         meta_sem,
+        res_sem,
         home_sem,
         g_send,
         g_recv,
-    ) = refs[:49]
+    ) = refs[:52]
     place = Place()
     me = place.me
     fs = lax.axis_index("fsdp")
@@ -307,8 +311,10 @@
 
     greet("exp", me, peers)
     greet("fsdp", fs, groups)
-    rest = refs[49:]
-    heads = [Reduce(place, r, send_v, rest[7 * i : 7 * i + 7]) for i, r in enumerate(ROUTES)]
+    rest = refs[52:]
+    heads = [
+        Reduce(place, r, send_v, rest[7 * i : 7 * i + 7]) for i, r in enumerate(HEAD_ROUTES)
+    ]
     rest = rest[7 * len(ROUTES) :]
     sums = [Reduce(place, r, part_v, rest[7 * i : 7 * i + 7]) for i, r in enumerate(ROUTES)]
     rest = rest[7 * len(ROUTES) :]
@@ -419,57 +425,56 @@
         for n in range(2):
             cache_copy(i, n).wait()
         each(route.first // 16, (route.first + route.count) // 16, attend)
-    for n in range(3):
-        weight_copy(n).start()
-
-    for i, route in enumerate(ROUTES):
         if i == 0:
-            out_copy.wait()
-            gain = jnp.zeros((1, depth), F32)
-            pad = jnp.zeros((wo_v.shape[0], WIDE - depth), BF)
-            res_pad = jnp.zeros((16, WIDE - depth), F32)
-            for j in range(peers):
-                part = slice(j * depth, (j + 1) * depth)
-                wo_s[j] = jnp.concatenate([wo_v[:, part], pad], axis=1)
-                res = jnp.concatenate([res_ref[0, :, part].astype(F32)] * 4, axis=0)
-                res_s[j] = jnp.concatenate([res, res_pad], axis=1)
-                gain = jnp.where(me == j, gain_ref[:, part], gain)
-            gain = jnp.concatenate([gain, jnp.zeros((1, WIDE - depth), F32)], axis=1)
-            lane = lax.broadcasted_iota(jnp.int32, (1, rows), 1)
-            here = lane // (STEPS * TOP) == lax.rem(me, 4)
-            own_ids = jnp.where(here, spread(ids_ref[0].astype(F32), rows), 0.0)
-            own_gates = jnp.where(here, spread(gates_ref[0], rows), 0.0)
-            meta_v[fs, me] = jnp.concatenate(
-                [own_ids, own_gates, jnp.zeros((6, rows), F32)], axis=0
-            )
-            pl.semaphore_wait(barrier, peers - 1 + groups - 1)
-        values = matmul(ctx_s[route.rows, :], wv_ref[...]).astype(BF)
-        owner = (route.first + lax.broadcasted_iota(jnp.int32, (route.count, 1), 0)) // STEPS
-        own_token = owner == me
-        together = 4 // route.line
-
-        def project(n, route=route, values=values, own_token=own_token, head=heads[i]):
-            spots = [(d, n * together + k) for k in range(together) for d in range(route.line)]
-            for d, g in spots:
-                j = place.plus(route.offset(d, g))
-                part = matmul(values, wo_s[j])
-                res = jnp.concatenate([res_s[j]] * (route.count // 16), axis=0)
-                send_v[j, route.rows, :] = (part + jnp.where(own_token, res, 0.0)).astype(BF)
-            for d, g in spots:
-                if d > 0:
-                    head.first(d, g).start()
-
-        each(0, route.plane // together, project)
-        if i == 0:
-            each(1, peers, lambda d: meta_copy(d).start())
+            for n in range(3):
+                weight_copy(n).start()
+
+    out_copy.wait()
+    for c in range(wo_v.shape[1] // 128):
+        span = slice(c * 128, c * 128 + 128)
+        wo_t[span, :] = wo_v[:, span].T
+    gain = jnp.zeros((1, depth), F32)
+    for j in range(peers):
+        part = slice(j * depth, (j + 1) * depth)
+        res_s[j, :, :depth] = res_ref[0, :, part].astype(F32)
+        gain = jnp.where(me == j, gain_ref[:, part], gain)
+    gain = jnp.concatenate([gain, jnp.zeros((1, WIDE - depth), F32)], axis=1)
+    lane = lax.broadcasted_iota(jnp.int32, (1, rows), 1)
+    here = lane // (STEPS * TOP) == lax.rem(me, 4)
+    own_ids = jnp.where(here, spread(ids_ref[0].astype(F32), rows), 0.0)
+    own_gates = jnp.where(here, spread(gates_ref[0], rows), 0.0)
+    meta_v[fs, me] = jnp.concatenate([own_ids, own_gates, jnp.zeros((6, rows), F32)], axis=0)
+    values = matmul(ctx_s[...], wv_ref[...]).astype(BF)
+    pl.semaphore_wait(barrier, peers - 1 + groups - 1)
+
+    def project(n):
+        offsets = [offset_of(4 * n + k) for k in range(4)]
+        for offset in offsets:
+            j = place.plus(offset)
+            span = pl.ds(pl.multiple_of(j * depth, 16), depth)
+            part = lax.dot_general(wo_t[span, :], values, NT, preferred_element_type=F32)
+            send_v[j] = part.astype(BF)
+        for offset in offsets:
+            for h in heads:
+                h.send(offset)
+
+    each(0, peers // 4, project)
+
+    def res_copy(d):
+        peer = lax.rem(me + d, peers)
+        return remote(res_s.at[peer], res_r.at[me], res_sem.at[0], res_sem.at[1], peer)
+
+    each(1, peers, lambda d: meta_copy(d).start())
+    each(1, peers, lambda d: res_copy(d).start())
+    res_r[me] = res_s[me]
 
     all_copies(meta_v.at[fs], meta_sem).wait_recv()
     for d in range(1, groups):
         group_copy(0, d, meta_v.at[fs]).start()
 
     for h in heads:
-        each(1, h.route.plane, lambda g, h=h: h.step(g, att))
-        h.step(0, att)
+        each(1, h.route.plane, lambda g, h=h: h.step(g, att_t))
+        h.step(0, att_t)
     pair_lane = lax.broadcasted_iota(jnp.int32, (1, rows), 1)
     slot_c = lax.broadcasted_iota(jnp.int32, (rows, experts * block), 1)
     slot_r = lax.broadcasted_iota(jnp.int32, (experts * block, rows), 0)
@@ -495,9 +500,14 @@
         group_copy(0, q, meta_v.at[from_group(q)]).wait_recv()
         read_meta(q)
     for h in heads:
-        h.add(att)
-
-    attended = att[...]
+        h.add(att_t)
+    all_copies(res_s, res_sem).wait_recv()
+
+    attended = jnp.concatenate([att_t[...], jnp.zeros((WIDE - depth, tokens), F32)], axis=0).T
+    own_res = jnp.concatenate([res_r[n][:, :depth] for n in range(peers)], axis=0)
+    own_res = jnp.concatenate([own_res, jnp.zeros((tokens, WIDE - depth), F32)], axis=1)
+    attended = attended + own_res
+    att[...] = attended
     x_v[fs] = (attended * gain).astype(BF)
     for d in range(1, groups):
         group_copy(1, d, x_v.at[fs]).start()
@@ -670,6 +680,7 @@
 
     all_copies(ssq_r, ssq_sem).wait_send()
     all_copies(meta_v.at[fs], meta_sem).wait_send()
+    all_copies(res_s, res_sem).wait_send()
     all_copies(home_s, home_sem).wait_recv()
     for j in range(peers):
         out_ref[0, :, j * depth : (j + 1) * depth] = home_r[j][:, :depth]
@@ -702,13 +713,15 @@
     scratch = [
         pltpu.VMEM((peers, experts * block, 2 * half), BF),
         pltpu.VMEM(w_out.shape[1:], BF),
-        pltpu.VMEM((peers, w_out.shape[1], WIDE), BF),
-        pltpu.VMEM((peers, 16, WIDE), F32),
+        pltpu.VMEM((w_out.shape[2], w_out.shape[1]), BF),
+        pltpu.VMEM((peers, steps, WIDE), F32),
+        pltpu.VMEM((peers, steps, WIDE), F32),
         pltpu.VMEM((tokens, key), BF),
         pltpu.VMEM((tokens, key), BF),
         pltpu.VMEM((tokens, tokens), F32),
         pltpu.VMEM((tokens, w_value.shape[1]), BF),
-        pltpu.VMEM((peers, tokens, WIDE), BF),
+        pltpu.VMEM((peers, depth, tokens), BF),
+        pltpu.VMEM((depth, tokens), F32),
         pltpu.VMEM((tokens, WIDE), F32),
         pltpu.VMEM((8, tokens), F32),
         pltpu.VMEM((peers, 8, tokens), F32),
@@ -733,11 +746,12 @@
         dma((2,)),
         dma((2,)),
         dma((2,)),
+        dma((2,)),
         dma((4, groups)),
         dma((4, groups)),
     ]
-    for route in ROUTES:
-        scratch += reduce_scratch(route, WIDE)
+    for route in HEAD_ROUTES:
+        scratch += reduce_scratch(route, tokens)
     for route in ROUTES:
         scratch += reduce_scratch(route, 2 * half)
     for route in ROUTES:

time: 124 us -> 124 us (level)
  no operation moved by 1% of the time
where the time goes in v6:
time: 124 us
  Pallas kernels  122 us (98%)
  local copies, waits for them, and re-layouts  1.55 us (1%)
    pallas_call x1, Pallas kernels, shards(): pl.pallas_call(functools.partial(layer_kernel, peers, groups), out_shape=...  122 us

profile of v6, /device:TPU:1, one launch (start us, length us, event | category | flops | bytes accessed | tf_op | source)
XLA Modules:
  0.0 124.0 jit_solution(13675887586884260270)
XLA Ops:
  0.0 122.4 %layer.1 = f32[1,4,7168]{2,1,0:T(4,128)} custom-call(s32[32]{0:T(128)} %refs_0_.1, bf16[32,4,576]{2,1,0:T(4,128)(2,1)} %bitcast.5, bf16[32,4,576]{2,1,0:T(4,128)(2,1)} %refs_2_.1, bf16[32,576,256]{2,1,0:T(8,128)(2,1)} %refs_3_.1, bf16[512,128]{1,0:T(8,128)(2,1)} %bitcast.6, bf16[128,7168]{1,0:T(8,128)(2,1)} %bitcast.4, bf16[1,4,7168]{2,1,0:T(4,128)(2,1)} %refs_6_.1, ...), custom_call_target="tpu_custom_call" | custom-call | tf_op jit(solution)/shard_map/layer/pallas_call | solution.py:759
  122.4 1.6 %copy.15 = f32[1,4,7168]{2,1,0:T(4,128)} copy(f32[1,4,7168]{2,1,0:T(4,128)} %layer.1) | data formatting | bytes 229376

commit v7 on v6

--- a/solution.py
+++ b/solution.py
@@ -60,30 +60,24 @@
 
 class Route:
     def __init__(self, kind, first, count):
-        self.kind = kind
+        self.axes = {"z": (1, 2, 0), "y": (2, 0, 1), "x": (0, 1, 2)}[kind]
+        self.n = tuple((NX, NZ, NY)[a] for a in self.axes)
         self.first, self.count = first, count
         self.rows = pl.ds(first, count)
-        self.line = NX if kind == "x" else NZ
-        self.plane = NX * NZ * NY // self.line
-
-    def offset(self, d, g):
-        if self.kind == "z":
-            return (g // NY, d, lax.rem(g, NY))
-        if self.kind == "y":
-            return (g // NZ, lax.rem(g, NZ), d)
-        return (d, g // NY, lax.rem(g, NY))
+        self.plane = self.n[1] * self.n[2]
+
+    def offset(self, d1, d2, d3):
+        out = [0, 0, 0]
+        for a, d in zip(self.axes, (d1, d2, d3)):
+            out[a] = d
+        return tuple(out)
 
     def split(self, offset):
-        dx, dz, dy = offset
-        if self.kind == "z":
-            return dz, dx * NY + dy
-        if self.kind == "y":
-            return dy, dx * NZ + dz
-        return dx, dz * NY + dy
-
-
-ROUTES = (Route("z", 0, 48), Route("y", 48, 48), Route("x", 96, 32))
-HEAD_ROUTES = (Route("z", 0, 80), Route("y", 80, 80), Route("x", 160, 64))
+        return tuple(offset[a] for a in self.axes)
+
+
+ROUTES = (Route("z", 0, 32), Route("y", 32, 48), Route("x", 80, 48))
+HEAD_ROUTES = (Route("z", 0, 64), Route("y", 64, 80), Route("x", 144, 80))
 
 
 def remote(src, dst, send, recv, peer):
@@ -100,127 +94,164 @@
 class Reduce:
     def __init__(self, place, route, src, bufs):
         self.place, self.route, self.src = place, route, src
-        self.got, self.out, self.fin, self.s1, self.r1, self.s2, self.r2 = bufs
-
-    def first(self, d, g):
+        self.got1, self.out1, self.got2, self.keep, self.out2, self.got3 = bufs[:6]
+        self.sent, self.r1, self.r2 = bufs[6:]
+
+    def first(self, d1, d2, d3):
         route = self.route
+        g = d2 * route.n[2] + d3
         return remote(
-            self.src.at[self.place.plus(route.offset(d, g)), route.rows],
-            self.got.at[g, d - 1],
-            self.s1,
+            self.src.at[self.place.plus(route.offset(d1, d2, d3)), route.rows],
+            self.got1.at[g, d1 - 1],
+            self.sent.at[0],
             self.r1.at[g],
-            self.place.plus(route.offset(d, 0)),
+            self.place.plus(route.offset(d1, 0, 0)),
         )
 
-    def second(self, g):
+    def second(self, d2, d3):
         return remote(
-            self.out.at[g],
-            self.fin.at[g],
-            self.s2,
-            self.r2,
-            self.place.plus(self.route.offset(0, g)),
+            self.out1.at[d2 * self.route.n[2] + d3],
+            self.got2.at[d3, d2 - 1],
+            self.sent.at[1],
+            self.r2.at[d3],
+            self.place.plus(self.route.offset(0, d2, 0)),
         )
 
+    def third(self, d3):
+        return remote(
+            self.out2.at[d3],
+            self.got3.at[d3 - 1],
+            self.sent.at[2],
+            self.r2.at[self.route.n[2]],
+            self.place.plus(self.route.offset(0, 0, d3)),
+        )
+
     def send(self, offset):
-        d, g = self.route.split(offset)
-
-        @pl.when(d > 0)
+        d1, d2, d3 = self.route.split(offset)
+
+        @pl.when(d1 > 0)
         def _():
-            self.first(d, g).start()
-
-    def step(self, g, acc_ref):
+            self.first(d1, d2, d3).start()
+
+    def arrived(self, got, sem):
+        remote(got, got, self.sent.at[0], sem, self.place.me).wait_recv()
+
+    def step(self, g):
         route = self.route
-        got = self.got.at[g]
-        remote(got, got, self.s1, self.r1.at[g], self.place.me).wait_recv()
-        total = self.src[self.place.plus(route.offset(0, g)), route.rows].astype(F32)
-        for d in range(1, route.line):
-            total = total + self.got[g, d - 1].astype(F32)
-
-        @pl.when(g == 0)
+        d2, d3 = g // route.n[2], lax.rem(g, route.n[2])
+        self.arrived(self.got1.at[g], self.r1.at[g])
+        total = self.src[self.place.plus(route.offset(0, d2, d3)), route.rows].astype(F32)
+        for d in range(1, route.n[0]):
+            total = total + self.got1[g, d - 1].astype(F32)
+
+        @pl.when(d2 == 0)
         def _():
-            acc_ref[route.rows] = total
-
-        @pl.when(g != 0)
+            self.keep[d3] = total
+
+        @pl.when(d2 != 0)
         def _():
-            self.out[g] = total.astype(BF)
-            self.second(g).start()
+            self.out1[g] = total.astype(BF)
+            self.second(d2, d3).start()
+
+    def turn(self, d3):
+        self.arrived(self.got2.at[d3], self.r2.at[d3])
+        total = self.keep[d3]
+        for d in range(1, self.route.n[1]):
+            total = total + self.got2[d3, d - 1].astype(F32)
+        return total
+
+    def turns(self):
+        for d3 in range(1, self.route.n[2]):
+            self.out2[d3] = self.turn(d3).astype(BF)
+            self.third(d3).start()
+        self.keep[0] = self.turn(0)
 
     def add(self, acc_ref):
-        route = self.route
-        rest = self.fin.at[pl.ds(1, route.plane - 1)]
-        remote(rest, rest, self.s2, self.r2, self.place.me).wait_recv()
-        total = acc_ref[route.rows]
-        for g in range(1, route.plane):
-            total = total + self.fin[g].astype(F32)
-        acc_ref[route.rows] = total
+        self.arrived(self.got3, self.r2.at[self.route.n[2]])
+        total = self.keep[0]
+        for d in range(1, self.route.n[2]):
+            total = total + self.got3[d - 1].astype(F32)
+        acc_ref[self.route.rows] = total
 
     def finish(self):
-        rest = self.out.at[pl.ds(1, self.route.plane - 1)]
-        remote(self.got, self.got, self.s1, self.r1.at[0], self.place.me).wait_send()
-        remote(rest, rest, self.s2, self.r2, self.place.me).wait_send()
+        for n, got in enumerate((self.got1, self.got2, self.got3)):
+            remote(got, got, self.sent.at[n], self.r2.at[0], self.place.me).wait_send()
 
 
 def reduce_scratch(route, cols):
-    lines, plane = route.line - 1, route.plane
+    n1, n2, n3 = route.n
     dma = pltpu.SemaphoreType.DMA
     return [
-        pltpu.VMEM((plane, lines, route.count, cols), BF),
-        pltpu.VMEM((plane, route.count, cols), BF),
-        pltpu.VMEM((plane, route.count, cols), BF),
-        dma,
-        dma((plane,)),
-        dma,
-        dma,
+        pltpu.VMEM((n2 * n3, n1 - 1, route.count, cols), BF),
+        pltpu.VMEM((n2 * n3, route.count, cols), BF),
+        pltpu.VMEM((n3, n2 - 1, route.count, cols), BF),
+        pltpu.VMEM((n3, route.count, cols), F32),
+        pltpu.VMEM((n3, route.count, cols), BF),
+        pltpu.VMEM((n3 - 1, route.count, cols), BF),
+        dma((3,)),
+        dma((n2 * n3,)),
+        dma((n3 + 1,)),
     ]
 
 
 class Gather:
     def __init__(self, place, route, whole, bufs):
         self.place, self.route, self.whole = place, route, whole
-        self.s1, self.s2, self.r = bufs
-
-    def near(self, g, source):
+        self.sent, self.r = bufs
+
+    def copy(self, source, to, offset):
+        _, n2, n3 = self.route.n
+        d1, d2, d3 = offset
         block = self.whole.at[source, self.route.rows]
-        return remote(
-            block, block, self.s1, self.r.at[0, g], self.place.plus(self.route.offset(0, g))
-        )
-
-    def far(self, d, g, source):
-        block = self.whole.at[source, self.route.rows]
-        return remote(
-            block, block, self.s2, self.r.at[d, g], self.place.plus(self.route.offset(d, 0))
-        )
+        peer = self.place.plus(self.route.offset(*to))
+        return remote(block, block, self.sent, self.r.at[(d1 * n2 + d2) * n3 + d3], peer)
+
+    def source(self, *offset):
+        return self.place.minus(self.route.offset(*offset))
+
+    def push1(self, d2, d3):
+        for d in range(1, self.route.n[0]):
+            self.copy(self.source(0, d2, d3), (d, 0, 0), (d, d2, d3)).start()
+
+    def push2(self, d3):
+        for d in range(1, self.route.n[1]):
+            self.copy(self.source(0, 0, d3), (0, d, 0), (0, d, d3)).start()
 
     def begin(self):
-        each(1, self.route.plane, lambda g: self.near(g, self.place.me).start())
-        self.forward(0)
-
-    def forward(self, g):
-        source = self.place.minus(self.route.offset(0, g))
-        for d in range(1, self.route.line):
-            self.far(d, g, source).start()
-
-    def relay(self, g):
-        self.near(g, self.place.minus(self.route.offset(0, g))).wait_recv()
-        self.forward(g)
+        for d in range(1, self.route.n[2]):
+            self.copy(self.place.me, (0, 0, d), (0, 0, d)).start()
+        self.push2(0)
+        self.push1(0, 0)
+
+    def wait(self, offset):
+        self.copy(self.source(*offset), (0, 0, 0), offset).wait_recv()
+
+    def relay_last(self, d3):
+        self.wait((0, 0, d3))
+        self.push2(d3)
+        self.push1(0, d3)
+
+    def relay_middle(self, g):
+        d2, d3 = g // self.route.n[2], lax.rem(g, self.route.n[2])
+        self.wait((0, d2, d3))
+        self.push1(d2, d3)
 
     def arrive(self, offset):
-        d, g = self.route.split(offset)
-
-        @pl.when(d > 0)
+        split = self.route.split(offset)
+
+        @pl.when(split[0] > 0)
         def _():
-            self.far(d, g, self.place.minus(offset)).wait_recv()
+            self.wait(split)
 
     def finish(self):
-        route = self.route
-        for sem, count in ((self.s1, route.plane - 1), (self.s2, (route.line - 1) * route.plane)):
-            blocks = self.whole.at[pl.ds(0, count), route.rows]
-            remote(blocks, blocks, sem, self.r.at[0, 0], self.place.me).wait_send()
+        n1, n2, n3 = self.route.n
+        blocks = self.whole.at[pl.ds(0, n1 * n2 * n3 - 1), self.route.rows]
+        remote(blocks, blocks, self.sent, self.r.at[0], self.place.me).wait_send()
 
 
 def gather_scratch(route):
     dma = pltpu.SemaphoreType.DMA
-    return [dma, dma, dma((route.line, route.plane))]
+    return [dma, dma((route.n[0] * route.n[1] * route.n[2],))]
 
 
 def offset_of(o):
@@ -313,12 +344,12 @@
     greet("fsdp", fs, groups)
     rest = refs[52:]
     heads = [
-        Reduce(place, r, send_v, rest[7 * i : 7 * i + 7]) for i, r in enumerate(HEAD_ROUTES)
+        Reduce(place, r, send_v, rest[9 * i : 9 * i + 9]) for i, r in enumerate(HEAD_ROUTES)
     ]
-    rest = rest[7 * len(ROUTES) :]
-    sums = [Reduce(place, r, part_v, rest[7 * i : 7 * i + 7]) for i, r in enumerate(ROUTES)]
-    rest = rest[7 * len(ROUTES) :]
-    gathers = [Gather(place, r, hid_v, rest[3 * i : 3 * i + 3]) for i, r in enumerate(ROUTES)]
+    rest = rest[9 * len(ROUTES) :]
+    sums = [Reduce(place, r, part_v, rest[9 * i : 9 * i + 9]) for i, r in enumerate(ROUTES)]
+    rest = rest[9 * len(ROUTES) :]
+    gathers = [Gather(place, r, hid_v, rest[2 * i : 2 * i + 2]) for i, r in enumerate(ROUTES)]
 
     def group_copy(n, d, block_ref):
         return pltpu.make_async_remote_copy(
@@ -473,8 +504,9 @@
         group_copy(0, d, meta_v.at[fs]).start()
 
     for h in heads:
-        each(1, h.route.plane, lambda g, h=h: h.step(g, att_t))
-        h.step(0, att_t)
+        each(h.route.n[2], h.route.plane, h.step)
+    for h in heads:
+        each(0, h.route.n[2], h.step)
     pair_lane = lax.broadcasted_iota(jnp.int32, (1, rows), 1)
     slot_c = lax.broadcasted_iota(jnp.int32, (rows, experts * block), 1)
     slot_r = lax.broadcasted_iota(jnp.int32, (experts * block, rows), 0)
@@ -496,6 +528,8 @@
         each(0, per, one)
 
     read_meta(0)
+    for h in heads:
+        h.turns()
     for q in range(1, groups):
         group_copy(0, q, meta_v.at[from_group(q)]).wait_recv()
         read_meta(q)
@@ -563,13 +597,13 @@
 
         @pl.when(lax.rem(p, 2) == place.z // 2)
         def _():
-            each(0, NY, lambda i: sums[0].step(x_off * NY + i, acc))
-
-        each(0, 2, lambda i: sums[1].step(x_off * NZ + z_off(i), acc))
+            each(0, NY, lambda i: sums[0].step(i * NX + x_off))
+
+        each(0, 2, lambda i: sums[1].step(x_off * NZ + z_off(i)))
 
         @pl.when(x_off == 0)
         def _():
-            each(0, 2 * NY, lambda i: sums[2].step(z_off(i // NY) * NY + lax.rem(i, NY), acc))
+            each(0, 2 * NY, lambda i: sums[2].step(z_off(i // NY) * NY + lax.rem(i, NY)))
 
     weight_copy(0).wait()
     weight_copy(1).wait()
@@ -593,6 +627,8 @@
     relay(3)
 
     for s in sums:
+        s.turns()
+    for s in sums:
         s.add(acc)
 
     for d in range(1, groups):
@@ -608,7 +644,10 @@
     for g in gathers:
         g.begin()
     for g in gathers:
-        each(1, g.route.plane, g.relay)
+        for d3 in range(1, g.route.n[2]):
+            g.relay_last(d3)
+    for g in gathers:
+        each(g.route.n[2], g.route.plane, g.relay_middle)
 
     def expand(n):
         offsets = [offset_of(2 * n), offset_of(2 * n + 1)]

time: 124 us -> 123 us (level)
  no operation moved by 1% of the time
where the time goes in v7:
time: 123 us
  Pallas kernels  122 us (99%)
  local copies, waits for them, and re-layouts  1.55 us (1%)
    pallas_call x1, Pallas kernels, shards(): pl.pallas_call(functools.partial(layer_kernel, peers, groups), out_shape=...  122 us

profile of v7, /device:TPU:1, one launch (start us, length us, event | category | flops | bytes accessed | tf_op | source)
XLA Modules:
  0.0 123.1 jit_solution(14173060997163260579)
XLA Ops:
  0.0 121.5 %layer.1 = f32[1,4,7168]{2,1,0:T(4,128)} custom-call(s32[32]{0:T(128)} %refs_0_.1, bf16[32,4,576]{2,1,0:T(4,128)(2,1)} %bitcast.5, bf16[32,4,576]{2,1,0:T(4,128)(2,1)} %refs_2_.1, bf16[32,576,256]{2,1,0:T(8,128)(2,1)} %refs_3_.1, bf16[512,128]{1,0:T(8,128)(2,1)} %bitcast.6, bf16[128,7168]{1,0:T(8,128)(2,1)} %bitcast.4, bf16[1,4,7168]{2,1,0:T(4,128)(2,1)} %refs_6_.1, ...), custom_call_target="tpu_custom_call" | custom-call | tf_op jit(solution)/shard_map/layer/pallas_call | solution.py:798
  121.5 1.6 %copy.15 = f32[1,4,7168]{2,1,0:T(4,128)} copy(f32[1,4,7168]{2,1,0:T(4,128)} %layer.1) | data formatting | bytes 229376

commit v8 on v7

--- a/solution.py
+++ b/solution.py
@@ -499,10 +499,6 @@
     each(1, peers, lambda d: res_copy(d).start())
     res_r[me] = res_s[me]
 
-    all_copies(meta_v.at[fs], meta_sem).wait_recv()
-    for d in range(1, groups):
-        group_copy(0, d, meta_v.at[fs]).start()
-
     for h in heads:
         each(h.route.n[2], h.route.plane, h.step)
     for h in heads:
@@ -527,12 +523,12 @@
 
         each(0, per, one)
 
-    read_meta(0)
     for h in heads:
         h.turns()
-    for q in range(1, groups):
-        group_copy(0, q, meta_v.at[from_group(q)]).wait_recv()
-        read_meta(q)
+    all_copies(meta_v.at[fs], meta_sem).wait_recv()
+    for d in range(1, groups):
+        group_copy(0, d, meta_v.at[fs]).start()
+    read_meta(0)
     for h in heads:
         h.add(att_t)
     all_copies(res_s, res_sem).wait_recv()
@@ -610,12 +606,10 @@
     multiply(0, per, x_v[fs][:, :depth])
     pick_group(0)
 
-    all_copies(ssq_r.at[pl.ds(1, peers - 1)], ssq_sem).wait_recv()
-    sum_v[fs] = jnp.sum(ssq_r[...], axis=0)
-    for d in range(1, groups):
-        group_copy(2, d, sum_v.at[fs]).start()
     for q in range(1, groups):
+        group_copy(0, q, meta_v.at[from_group(q)]).wait_recv()
         group_copy(1, q, x_v.at[from_group(q)]).wait_recv()
+        read_meta(q)
     others = [x_v[from_group(q)][:, :depth] for q in range(1, groups)]
     multiply(per, peers - per, jnp.concatenate(others, axis=0))
     pick_group(1)
@@ -623,6 +617,10 @@
     pick_group(2)
     relay(1)
     pick_group(3)
+    all_copies(ssq_r.at[pl.ds(1, peers - 1)], ssq_sem).wait_recv()
+    sum_v[fs] = jnp.sum(ssq_r[...], axis=0)
+    for d in range(1, groups):
+        group_copy(2, d, sum_v.at[fs]).start()
     relay(2)
     relay(3)
 

time: 123 us -> 115 us (0.935)
  Pallas kernels: 122 us -> 113 us
    pallas_call x1, Pallas kernels: 122 us -> 113 us  [shards(): pl.pallas_call(functools.partial(layer_kernel, peers, groups), out_shape=...]
where the time goes in v8:
time: 115 us
  Pallas kernels  113 us (98%)
  local copies, waits for them, and re-layouts  1.55 us (1%)
    pallas_call x1, Pallas kernels, shards(): pl.pallas_call(functools.partial(layer_kernel, peers, groups), out_shape=...  113 us

profile of v8, /device:TPU:1, one launch (start us, length us, event | category | flops | bytes accessed | tf_op | source)
XLA Modules:
  0.0 114.7 jit_solution(15901145220844642526)
XLA Ops:
  0.0 113.1 %layer.1 = f32[1,4,7168]{2,1,0:T(4,128)} custom-call(s32[32]{0:T(128)} %refs_0_.1, bf16[32,4,576]{2,1,0:T(4,128)(2,1)} %bitcast.5, bf16[32,4,576]{2,1,0:T(4,128)(2,1)} %refs_2_.1, bf16[32,576,256]{2,1,0:T(8,128)(2,1)} %refs_3_.1, bf16[512,128]{1,0:T(8,128)(2,1)} %bitcast.6, bf16[128,7168]{1,0:T(8,128)(2,1)} %bitcast.4, bf16[1,4,7168]{2,1,0:T(4,128)(2,1)} %refs_6_.1, ...), custom_call_target="tpu_custom_call" | custom-call | tf_op jit(solution)/shard_map/layer/pallas_call | solution.py:796
  113.1 1.6 %copy.15 = f32[1,4,7168]{2,1,0:T(4,128)} copy(f32[1,4,7168]{2,1,0:T(4,128)} %layer.1) | data formatting | bytes 229376

commit v9 on v8

--- a/solution.py
+++ b/solution.py
@@ -210,7 +210,7 @@
         return self.place.minus(self.route.offset(*offset))
 
     def push1(self, d2, d3):
-        for d in range(1, self.route.n[0]):
+        for d in sorted(range(1, self.route.n[0]), key=lambda d: d != 2):
             self.copy(self.source(0, d2, d3), (d, 0, 0), (d, d2, d3)).start()
 
     def push2(self, d3):
@@ -254,8 +254,20 @@
     return [dma, dma((route.n[0] * route.n[1] * route.n[2],))]
 
 
+def offset_of_int(o):
+    return (o // (NZ * NY), o // NY % NZ, o % NY)
+
+
 def offset_of(o):
     return (o // (NZ * NY), lax.rem(o // NY, NZ), lax.rem(o, NY))
+
+
+def hops(offset):
+    dx, dz, dy = offset
+    return 2 * dx + min(dz, NZ - dz) + min(dy, NY - dy)
+
+
+FAR_FIRST = sorted((offset_of_int(o) for o in range(1, NX * NZ * NY)), key=hops, reverse=True)
 
 
 def spread(block, lanes):
@@ -305,6 +317,7 @@
         acc,
         hid_v,
         spread_s,
+        code_s,
         gate_s,
         routed_v,
         routed_r,
@@ -319,7 +332,7 @@
         home_sem,
         g_send,
         g_recv,
-    ) = refs[:52]
+    ) = refs[:53]
     place = Place()
     me = place.me
     fs = lax.axis_index("fsdp")
@@ -342,7 +355,7 @@
 
     greet("exp", me, peers)
     greet("fsdp", fs, groups)
-    rest = refs[52:]
+    rest = refs[53:]
     heads = [
         Reduce(place, r, send_v, rest[9 * i : 9 * i + 9]) for i, r in enumerate(HEAD_ROUTES)
     ]
@@ -446,7 +459,7 @@
 
     def meta_copy(d):
         tile = meta_v.at[fs, me]
-        return remote(tile, tile, meta_sem.at[0], meta_sem.at[1], lax.rem(me + d, peers))
+        return remote(tile, tile, meta_sem.at[0], meta_sem.at[1], place.plus(d))
 
     def all_copies(buffer, sem):
         tiles = buffer.at[pl.ds(0, peers - 1)]
@@ -492,11 +505,12 @@
     each(0, peers // 4, project)
 
     def res_copy(d):
-        peer = lax.rem(me + d, peers)
+        peer = place.plus(d)
         return remote(res_s.at[peer], res_r.at[me], res_sem.at[0], res_sem.at[1], peer)
 
-    each(1, peers, lambda d: meta_copy(d).start())
-    each(1, peers, lambda d: res_copy(d).start())
+    for d in FAR_FIRST:
+        meta_copy(d).start()
+        res_copy(d).start()
     res_r[me] = res_s[me]
 
     for h in heads:
@@ -516,7 +530,7 @@
                 info = info + meta_v[piece, 4 * n + i]
             j = piece * per + n
             code = info[0:1, :].astype(jnp.int32) * block + pair_lane // TOP
-            spread_s[j] = (code == slot_r).astype(F32).astype(BF)
+            code_s[j] = code
             code = jnp.sum(jnp.where(diagonal, code, 0), 1, keepdims=True)
             part_v[j] = (code == slot_c).astype(F32).astype(BF)
             gate_s[j] = info[1:2, :]
@@ -626,6 +640,12 @@
 
     for s in sums:
         s.turns()
+
+    def build(n):
+        for j in (2 * n, 2 * n + 1):
+            spread_s[j] = (code_s[j] == slot_r).astype(F32).astype(BF)
+
+    each(0, peers // 2, build)
     for s in sums:
         s.add(acc)
 
@@ -702,10 +722,11 @@
         home_s[j, :, :depth] = mixed[j * own_rows : (j + 1) * own_rows, :]
 
     def home_copy(d):
-        peer = lax.rem(me + d, peers)
+        peer = place.plus(d)
         return remote(home_s.at[peer], home_r.at[me], home_sem.at[0], home_sem.at[1], peer)
 
-    each(1, peers, lambda d: home_copy(d).start())
+    for d in FAR_FIRST:
+        home_copy(d).start()
     home_r[me] = home_s[me]
     for s in heads + sums + gathers:
         s.finish()
@@ -772,6 +793,7 @@
         pltpu.VMEM((rows, 2 * half), F32),
         pltpu.VMEM((peers, rows, half), BF),
         pltpu.VMEM((peers, experts * block, rows), BF),
+        pltpu.VMEM((peers, 1, rows), jnp.int32),
         pltpu.VMEM((peers, 1, rows), F32),
         pltpu.VMEM((groups, tokens, WIDE), BF),
         pltpu.VMEM((groups, tokens, WIDE), BF),

time: 115 us -> 115 us (level)
  no operation moved by 1% of the time
where the time goes in v9:
time: 115 us
  Pallas kernels  113 us (98%)
  local copies, waits for them, and re-layouts  1.55 us (1%)
    pallas_call x1, Pallas kernels, shards(): pl.pallas_call(functools.partial(layer_kernel, peers, groups), out_shape=...  113 us

profile of v9, /device:TPU:1, one launch (start us, length us, event | category | flops | bytes accessed | tf_op | source)
XLA Modules:
  0.0 114.9 jit_solution(10966356486560574914)
XLA Ops:
  0.0 113.4 %layer.1 = f32[1,4,7168]{2,1,0:T(4,128)} custom-call(s32[32]{0:T(128)} %refs_0_.1, bf16[32,4,576]{2,1,0:T(4,128)(2,1)} %bitcast.5, bf16[32,4,576]{2,1,0:T(4,128)(2,1)} %refs_2_.1, bf16[32,576,256]{2,1,0:T(8,128)(2,1)} %refs_3_.1, bf16[512,128]{1,0:T(8,128)(2,1)} %bitcast.6, bf16[128,7168]{1,0:T(8,128)(2,1)} %bitcast.4, bf16[1,4,7168]{2,1,0:T(4,128)(2,1)} %refs_6_.1, ...), custom_call_target="tpu_custom_call" | custom-call | tf_op jit(solution)/shard_map/layer/pallas_call | solution.py:818
  113.4 1.6 %copy.15 = f32[1,4,7168]{2,1,0:T(4,128)} copy(f32[1,4,7168]{2,1,0:T(4,128)} %layer.1) | data formatting | bytes 229376

commit v10 on v9

--- a/solution.py
+++ b/solution.py
@@ -377,6 +377,12 @@
     def from_group(d):
         return lax.rem(fs + groups - d, groups)
 
+    def turn_of(q):
+        return q + lax.rem(q, 2) * (2 - q) * 2 * (1 - lax.rem(fs, 2))
+
+    def piece_of(q):
+        return from_group(turn_of(q))
+
     def cache_copy(i, n):
         span = pl.ds(ROUTES[i].first // STEPS, ROUTES[i].count // STEPS)
         positions = cache_ref.shape[2]
@@ -522,7 +528,7 @@
     slot_r = lax.broadcasted_iota(jnp.int32, (experts * block, rows), 0)
 
     def read_meta(q):
-        piece = from_group(q)
+        piece = piece_of(q)
 
         def one(n):
             info = meta_v[piece, 4 * n]
@@ -581,7 +587,7 @@
         for k in range(2):
             q = (2 * i + k) // per
             n = lax.rem((2 * i + k) // NY, 2) * NY + lax.rem(place.y + 2 * i + k, NY)
-            j = from_group(q) * per + n
+            j = piece_of(q) * per + n
             found.append((j, matmul(part_v[j], dense[q * per + n]).astype(BF)))
         for j, part in found:
             part_v[j] = part
@@ -598,7 +604,7 @@
         each(q * per // 2, (q + 1) * per // 2, pick)
 
     def relay(q):
-        p = from_group(q)
+        p = piece_of(q)
         x_off = lax.rem(p // 2 + NX - place.x, NX)
         z_low = 2 * lax.rem(p, 2)
 
@@ -615,22 +621,28 @@
         def _():
             each(0, 2 * NY, lambda i: sums[2].step(z_off(i // NY) * NY + lax.rem(i, NY)))
 
+    def receive(q):
+        group_copy(0, turn_of(q), meta_v.at[piece_of(q)]).wait_recv()
+        group_copy(1, turn_of(q), x_v.at[piece_of(q)]).wait_recv()
+        read_meta(q)
+
+    def two(q):
+        pair = [x_v[piece_of(n)][:, :depth] for n in (q, q + 1)]
+        multiply(q * per, 2 * per, jnp.concatenate(pair, axis=0))
+
     weight_copy(0).wait()
     weight_copy(1).wait()
-    multiply(0, per, x_v[fs][:, :depth])
+    receive(1)
+    two(0)
     pick_group(0)
-
-    for q in range(1, groups):
-        group_copy(0, q, meta_v.at[from_group(q)]).wait_recv()
-        group_copy(1, q, x_v.at[from_group(q)]).wait_recv()
-        read_meta(q)
-    others = [x_v[from_group(q)][:, :depth] for q in range(1, groups)]
-    multiply(per, peers - per, jnp.concatenate(others, axis=0))
     pick_group(1)
+    receive(2)
+    receive(3)
+    two(2)
+    pick_group(2)
     relay(0)
-    pick_group(2)
+    pick_group(3)
     relay(1)
-    pick_group(3)
     all_copies(ssq_r.at[pl.ds(1, peers - 1)], ssq_sem).wait_recv()
     sum_v[fs] = jnp.sum(ssq_r[...], axis=0)
     for d in range(1, groups):

time: 115 us -> 116 us (level)
  no operation moved by 1% of the time
where the time goes in v10:
time: 116 us
  Pallas kernels  114 us (98%)
  local copies, waits for them, and re-layouts  1.55 us (1%)
    pallas_call x1, Pallas kernels, shards(): pl.pallas_call(functools.partial(layer_kernel, peers, groups), out_shape=...  114 us

profile of v10, /device:TPU:1, one launch (start us, length us, event | category | flops | bytes accessed | tf_op | source)
XLA Modules:
  0.0 115.6 jit_solution(18092000401663112839)
XLA Ops:
  0.0 114.0 %layer.1 = f32[1,4,7168]{2,1,0:T(4,128)} custom-call(s32[32]{0:T(128)} %refs_0_.1, bf16[32,4,576]{2,1,0:T(4,128)(2,1)} %bitcast.5, bf16[32,4,576]{2,1,0:T(4,128)(2,1)} %refs_2_.1, bf16[32,576,256]{2,1,0:T(8,128)(2,1)} %refs_3_.1, bf16[512,128]{1,0:T(8,128)(2,1)} %bitcast.6, bf16[128,7168]{1,0:T(8,128)(2,1)} %bitcast.4, bf16[1,4,7168]{2,1,0:T(4,128)(2,1)} %refs_6_.1, ...), custom_call_target="tpu_custom_call" | custom-call | tf_op jit(solution)/shard_map/layer/pallas_call | solution.py:830
  114.0 1.6 %copy.15 = f32[1,4,7168]{2,1,0:T(4,128)} copy(f32[1,4,7168]{2,1,0:T(4,128)} %layer.1) | data formatting | bytes 229376

commit v11 on v9

--- a/solution.py
+++ b/solution.py
@@ -629,8 +629,8 @@
     pick_group(1)
     relay(0)
     pick_group(2)
+    pick_group(3)
     relay(1)
-    pick_group(3)
     all_copies(ssq_r.at[pl.ds(1, peers - 1)], ssq_sem).wait_recv()
     sum_v[fs] = jnp.sum(ssq_r[...], axis=0)
     for d in range(1, groups):
@@ -706,15 +706,17 @@
         )
 
     mixed = att[:, :depth]
-    for pair in ((2, 3), (1, 0)):
-        both = shares([lax.rem(fs + d, groups) for d in pair])
+    odd = lax.rem(fs, 2)
+    for pair in ((2, 3 - 2 * odd), (1 + 2 * odd, None)):
+        pieces = [fs if d is None else lax.rem(fs + d, groups) for d in pair]
+        both = shares(pieces)
         for k, d in enumerate(pair):
             share = both[k * tokens : (k + 1) * tokens]
-            if d > 0:
-                routed_v[lax.rem(fs + d, groups), :, :depth] = share.astype(BF)
+            if d is None:
+                mixed = mixed + share
+            else:
+                routed_v[pieces[k], :, :depth] = share.astype(BF)
                 routed_copy(d).start()
-            else:
-                mixed = mixed + share
     for d in range(1, groups):
         routed_copy(d).wait_recv()
         mixed = mixed + routed_r[d][:, :depth].astype(F32)

time: 115 us -> 116 us (level)
  Pallas kernels: 113 us -> 115 us
    pallas_call x1, Pallas kernels: 113 us -> 115 us  [shards(): pl.pallas_call(functools.partial(layer_kernel, peers, groups), out_shape=...]
where the time goes in v11:
time: 116 us
  Pallas kernels  115 us (99%)
  local copies, waits for them, and re-layouts  1.55 us (1%)
    pallas_call x1, Pallas kernels, shards(): pl.pallas_call(functools.partial(layer_kernel, peers, groups), out_shape=...  115 us

profile of v11, /device:TPU:1, one launch (start us, length us, event | category | flops | bytes accessed | tf_op | source)
XLA Modules:
  0.0 116.3 jit_solution(3612599781967948309)
XLA Ops:
  0.0 114.8 %layer.1 = f32[1,4,7168]{2,1,0:T(4,128)} custom-call(s32[32]{0:T(128)} %refs_0_.1, bf16[32,4,576]{2,1,0:T(4,128)(2,1)} %bitcast.5, bf16[32,4,576]{2,1,0:T(4,128)(2,1)} %refs_2_.1, bf16[32,576,256]{2,1,0:T(8,128)(2,1)} %refs_3_.1, bf16[512,128]{1,0:T(8,128)(2,1)} %bitcast.6, bf16[128,7168]{1,0:T(8,128)(2,1)} %bitcast.4, bf16[1,4,7168]{2,1,0:T(4,128)(2,1)} %refs_6_.1, ...), custom_call_target="tpu_custom_call" | custom-call | tf_op jit(solution)/shard_map/layer/pallas_call | solution.py:820
  114.8 1.6 %copy.15 = f32[1,4,7168]{2,1,0:T(4,128)} copy(f32[1,4,7168]{2,1,0:T(4,128)} %layer.1) | data formatting | bytes 229376

commit v12 on v9

--- a/solution.py
+++ b/solution.py
@@ -220,8 +220,6 @@
     def begin(self):
         for d in range(1, self.route.n[2]):
             self.copy(self.place.me, (0, 0, d), (0, 0, d)).start()
-        self.push2(0)
-        self.push1(0, 0)
 
     def wait(self, offset):
         self.copy(self.source(*offset), (0, 0, 0), offset).wait_recv()
@@ -661,6 +659,10 @@
 
     for g in gathers:
         g.begin()
+    for g in gathers:
+        g.push2(0)
+    for g in gathers:
+        g.push1(0, 0)
     for g in gathers:
         for d3 in range(1, g.route.n[2]):
             g.relay_last(d3)

time: 115 us -> 115 us (level)
  no operation moved by 1% of the time
where the time goes in v12:
time: 115 us; the launch traced here: 114 us
  Pallas kernels  113 us (98%)
  local copies, waits for them, and re-layouts  1.55 us (1%)
    pallas_call x1, Pallas kernels, shards(): pl.pallas_call(functools.partial(layer_kernel, peers, groups), out_shape=...  113 us

profile of v12, /device:TPU:1, one launch (start us, length us, event | category | flops | bytes accessed | tf_op | source)
XLA Modules:
  0.0 114.4 jit_solution(10557788150072049666)
XLA Ops:
  0.0 112.8 %layer.1 = f32[1,4,7168]{2,1,0:T(4,128)} custom-call(s32[32]{0:T(128)} %refs_0_.1, bf16[32,4,576]{2,1,0:T(4,128)(2,1)} %bitcast.5, bf16[32,4,576]{2,1,0:T(4,128)(2,1)} %refs_2_.1, bf16[32,576,256]{2,1,0:T(8,128)(2,1)} %refs_3_.1, bf16[512,128]{1,0:T(8,128)(2,1)} %bitcast.6, bf16[128,7168]{1,0:T(8,128)(2,1)} %bitcast.4, bf16[1,4,7168]{2,1,0:T(4,128)(2,1)} %refs_6_.1, ...), custom_call_target="tpu_custom_call" | custom-call | tf_op jit(solution)/shard_map/layer/pallas_call | solution.py:820
  112.8 1.6 %copy.15 = f32[1,4,7168]{2,1,0:T(4,128)} copy(f32[1,4,7168]{2,1,0:T(4,128)} %layer.1) | data formatting | bytes 229376
